TPU v7x, 768 devices: a whole 4x8x12 slice. The times are simulated.
768 devices in a mesh: row: 48 (over z, x), rep: 16 (over y, core).
Axes of the slice: x: 4, y: 8, z: 12, core: 2. Of those that a mesh axis runs over, the one named last changes fastest.
Arguments:
- left_blocks: float32 [48, 128, 4096], P('row', 'rep'), may hold values from -0.75 to 0.75
- right_blocks: float32 [48, 16, 64, 4096], P('row', 'rep'), may hold values from -0.6 to 0.6
- task_right: int32 [48, 16, 1024], P('row', 'rep'), may hold values from 0 to 63
- task_slot: int32 [48, 16, 1024], P('row', 'rep'), may hold values from 0 to 95, as said below
- recv_owner: int32 [48, 96], P('row'), may hold values from 0 to 31, as said below
Outputs:
- owned_blocks: float32 [48, 32, 4096], P('row', 'rep')
Inputs may be any that keep to these rules, and one draw needn't show every extreme that they name: `task_slot`: each device's list names every one of its 96 slots. `recv_owner`: each row index's list names every one of its 32 blocks.
All inputs are finite; a program needn't handle non-finite values.
Results may differ from a plain program's by a relative error of at most 0.0003.
Values sent between devices are 32-bit elements; how exact they have to be, the bound alone decides.
No kernel may reach another device: no remote copies, remote signals or barrier semaphores. Data moves between devices by JAX's collectives and lax.ppermute only.
A program may use at most 32 MiB of HBM per device.

v0:
```python
import jax
import jax.numpy as jnp
from jax import lax
from jax.sharding import PartitionSpec as P

BS = 64
OWN_DEV = 2


def add_products(totals, left_panel, offset, rights, picks, targets, per_block, slot_count):
    block_count = left_panel.shape[0]
    group_size = 16
    turns = block_count // group_size

    def advance(turn_index, running):
        left_group = lax.dynamic_slice_in_dim(left_panel, turn_index * group_size, group_size, 0)
        task_first = (offset + turn_index * group_size) * per_block
        chosen = lax.dynamic_slice_in_dim(picks, task_first, group_size * per_block, 0)
        aimed = lax.dynamic_slice_in_dim(targets, task_first, group_size * per_block, 0)
        right_rows = rights[chosen].reshape(group_size, per_block, BS, BS)
        products = jnp.einsum(
            "kij,ktjl->ktil",
            left_group.reshape(group_size, BS, BS),
            right_rows,
            precision=lax.Precision.HIGHEST,
        )
        products = products.reshape(group_size * per_block, BS * BS)
        return running + jax.ops.segment_sum(products, aimed, num_segments=slot_count)

    return lax.fori_loop(0, turns, advance, totals)


def local(left_blocks, right_blocks, task_right, task_slot, recv_owner):
    row_count = lax.axis_size("row")
    group_count = lax.axis_size("rep")
    slot_count = recv_owner.shape[1]
    capacity = slot_count // row_count
    left_local = left_blocks[0]
    rights = right_blocks[0, 0]
    picks = task_right[0, 0]
    targets = task_slot[0, 0]
    per_block = picks.shape[0] // (left_local.shape[0] * group_count)
    empty = jnp.zeros((slot_count, left_local.shape[1]), jnp.float32)
    panel = lax.all_gather(left_local, "rep", axis=0, tiled=True)
    slots = add_products(empty, panel, 0, rights, picks, targets, per_block, slot_count)
    entry_count = slots.shape[1]
    outgoing = slots.reshape(row_count, capacity, entry_count)
    incoming = lax.all_to_all(outgoing, "row", split_axis=0, concat_axis=0, tiled=True).reshape(
        slot_count, entry_count
    )
    owners = recv_owner[0]
    owned_ids = jnp.arange(OWN_DEV * group_count, dtype=jnp.int32)
    selector = (owners[None, :] == owned_ids[:, None]).astype(jnp.float32)
    owned = jnp.dot(
        selector, incoming, precision=lax.Precision.HIGHEST, preferred_element_type=jnp.float32
    )
    mine = lax.psum_scatter(owned, "rep", scatter_dimension=0, tiled=True)[None]
    return mine


def solution(mesh):
    in_specs = (
        P("row", "rep", None),
        P("row", "rep", None, None),
        P("row", "rep", None),
        P("row", "rep", None),
        P("row", None),
    )
    out_specs = P("row", "rep", None)
    return jax.shard_map(local, mesh=mesh, in_specs=in_specs, out_specs=out_specs, check_vma=False)
```

profile of v0, /device:TPU:1, one launch (start us, length us, event | category | flops | bytes accessed | tf_op | source)
XLA Modules:
  0.0 552.9 jit_solution(15111965601887343017)
XLA Ops:
  7.3 55.0 %all-gather.3.cloned.1.call-done = f32[1,128,4096]{2,1,0:T(8,128)} async-done(((f32[1,8,4096]{2,1,0:T(8,128)}), f32[1,128,4096]{2,1,0:T(8,128)}) %all-gather.3.cloned.1.call-update) | async-done | bytes 2097168 | tf_op jit(solution)/shard_map/all_gather | solution.py:44
  62.4 294.2 %while.15 = (s32[]{:T(128)}, f32[96,4096]{1,0:T(8,128)S(1)}, s32[1024]{0:T(1024)}, s32[1024]{0:T(1024)}, f32[64,4096]{1,0:T(8,128)}, /*index=5*/f32[128,4096]{1,...) while((s32[]{:T(128)}, f32[96,4096]{1,0:T(8,128)S(1)}, s32[1024]{0:T(1024)}, ...), condition=%wide.region_2.0_spmd, body=%wide.region_0.0_spmd.sunk | while | flops 403178880 | bytes 28581588 | solution.py:30
  73.6 9.8 %convolution_bitcast_fusion.2 = f32[16,8,64,64]{2,3,1,0:T(8,128)} fusion(f32[16,8,64,64]{3,2,1,0:T(8,128)} %reshape.71, f32[16,64,64,1]{2,1,0,3:T(8,128)S(1)} %reshape.72), kind=kOutput, calls=%fused_computation.2.clone.1 | convolution fusion | flops 402653184 | bytes 4456448 | tf_op jit(solution)/shard_map/while/body/eval_jaxpr/kij,ktjl->ktil/dot_general | solution.py:21
  83.4 5.3 copy.14
  88.8 4.8 reshape.73
  94.3 4.9 scatter_fusion
  110.4 9.8 %convolution_bitcast_fusion.2 = f32[16,8,64,64]{2,3,1,0:T(8,128)} fusion(f32[16,8,64,64]{3,2,1,0:T(8,128)} %reshape.71, f32[16,64,64,1]{2,1,0,3:T(8,128)S(1)} %reshape.72), kind=kOutput, calls=%fused_computation.2.clone.1 | convolution fusion | flops 402653184 | bytes 4456448 | tf_op jit(solution)/shard_map/while/body/eval_jaxpr/kij,ktjl->ktil/dot_general | solution.py:21
  120.2 5.3 copy.14
  131.1 4.9 scatter_fusion
  147.2 9.8 %convolution_bitcast_fusion.2 = f32[16,8,64,64]{2,3,1,0:T(8,128)} fusion(f32[16,8,64,64]{3,2,1,0:T(8,128)} %reshape.71, f32[16,64,64,1]{2,1,0,3:T(8,128)S(1)} %reshape.72), kind=kOutput, calls=%fused_computation.2.clone.1 | convolution fusion | flops 402653184 | bytes 4456448 | tf_op jit(solution)/shard_map/while/body/eval_jaxpr/kij,ktjl->ktil/dot_general | solution.py:21
  157.0 5.3 copy.14
  162.3 4.8 reshape.73
  167.8 4.9 scatter_fusion
  183.9 9.8 %convolution_bitcast_fusion.2 = f32[16,8,64,64]{2,3,1,0:T(8,128)} fusion(f32[16,8,64,64]{3,2,1,0:T(8,128)} %reshape.71, f32[16,64,64,1]{2,1,0,3:T(8,128)S(1)} %reshape.72), kind=kOutput, calls=%fused_computation.2.clone.1 | convolution fusion | flops 402653184 | bytes 4456448 | tf_op jit(solution)/shard_map/while/body/eval_jaxpr/kij,ktjl->ktil/dot_general | solution.py:21
  193.7 5.3 copy.14
  199.1 4.8 reshape.73
  204.6 4.9 scatter_fusion
  220.7 9.8 %convolution_bitcast_fusion.2 = f32[16,8,64,64]{2,3,1,0:T(8,128)} fusion(f32[16,8,64,64]{3,2,1,0:T(8,128)} %reshape.71, f32[16,64,64,1]{2,1,0,3:T(8,128)S(1)} %reshape.72), kind=kOutput, calls=%fused_computation.2.clone.1 | convolution fusion | flops 402653184 | bytes 4456448 | tf_op jit(solution)/shard_map/while/body/eval_jaxpr/kij,ktjl->ktil/dot_general | solution.py:21
  230.5 5.3 copy.14
  235.9 4.8 reshape.73
  241.4 4.9 scatter_fusion
  257.5 9.8 %convolution_bitcast_fusion.2 = f32[16,8,64,64]{2,3,1,0:T(8,128)} fusion(f32[16,8,64,64]{3,2,1,0:T(8,128)} %reshape.71, f32[16,64,64,1]{2,1,0,3:T(8,128)S(1)} %reshape.72), kind=kOutput, calls=%fused_computation.2.clone.1 | convolution fusion | flops 402653184 | bytes 4456448 | tf_op jit(solution)/shard_map/while/body/eval_jaxpr/kij,ktjl->ktil/dot_general | solution.py:21
  267.3 5.3 copy.14
  278.2 4.9 scatter_fusion
  294.3 9.8 %convolution_bitcast_fusion.2 = f32[16,8,64,64]{2,3,1,0:T(8,128)} fusion(f32[16,8,64,64]{3,2,1,0:T(8,128)} %reshape.71, f32[16,64,64,1]{2,1,0,3:T(8,128)S(1)} %reshape.72), kind=kOutput, calls=%fused_computation.2.clone.1 | convolution fusion | flops 402653184 | bytes 4456448 | tf_op jit(solution)/shard_map/while/body/eval_jaxpr/kij,ktjl->ktil/dot_general | solution.py:21
  304.1 5.3 copy.14
  314.9 4.9 scatter_fusion
  331.0 9.8 %convolution_bitcast_fusion.2 = f32[16,8,64,64]{2,3,1,0:T(8,128)} fusion(f32[16,8,64,64]{3,2,1,0:T(8,128)} %reshape.71, f32[16,64,64,1]{2,1,0,3:T(8,128)S(1)} %reshape.72), kind=kOutput, calls=%fused_computation.2.clone.1 | convolution fusion | flops 402653184 | bytes 4456448 | tf_op jit(solution)/shard_map/while/body/eval_jaxpr/kij,ktjl->ktil/dot_general | solution.py:21
  340.8 5.3 copy.14
  351.7 4.9 scatter_fusion
  357.5 69.0 %all_to_all.5 = f32[48,2,4096]{2,1,0:T(2,128)S(1)} all-to-all(f32[48,2,4096]{2,1,0:T(2,128)S(1)} %reshape.36), channel_id=1, replica_groups=mesh['row'=48,'rep'=16] {'row'}, dimensions={0} | all-to-all | bytes 3145728 | tf_op jit(solution)/shard_map/all_to_all | solution.py:48
  431.1 113.4 %all-reduce.3.cloned.1.call-done = f32[32,4096]{1,0:T(8,128)} async-done(((f32[32,4096]{1,0:T(8,128)}), f32[32,4096]{1,0:T(8,128)}) %all-reduce.3.cloned.1.call-update) | async-done | bytes 524304
  (72 shorter events, 121.9 us)
Async XLA Ops:
  6.5 55.7 %all-gather.3.cloned.1.call-start = ((), (), s32[]{:S(2)}) async-start(), calls=%async_computation.1 | async-start | bytes 2228224 | tf_op jit(solution)/shard_map/all_gather | solution.py:44
  7.3 537.2 %all-reduce.3.cloned.1.call-start = ((), (), s32[]{:S(2)}) async-start(), calls=%async_computation.2 | async-start | bytes 1048576
  426.6 1.1 copy-start
Sparse Core Ops, SparseCore 0:
  9.8 52.4 all-gather.2
  429.3 115.1 all-reduce.2
where the time goes:
time: 556 us; the launch traced here: 553 us
  local copies, waits for them, and re-layouts  175 us (31%)
  waiting for transfers between devices  169 us (30%)
  matrix products  79.9 us (14%)
  blocking collectives  69 us (12%)
  other arithmetic  45.1 us (8%)
  between operations  14.1 us (3%)
    unnamed x3, waiting for transfers between devices  114 us
    dot_general x8, matrix products, advance(): jnp.einsum('kij,ktjl->ktil', left_group.reshape(group_size, BS, BS), righ...  78.4 us
    all_to_all x1, blocking collectives, local(): lax.all_to_all(outgoing, 'row', split_axis=0, concat_axis=0, tiled=True)  69 us
    all_gather x1, waiting for transfers between devices, local(): panel = lax.all_gather(left_local, 'rep', axis=0, tiled=True)  55 us
    transpose x8, local copies, waits for them, and re-layouts, advance(): jnp.einsum('kij,ktjl->ktil', left_group.reshape(group_size, BS, BS), righ...  42.7 us
    scatter-add x8, other arithmetic, advance(): jax.ops.segment_sum(products, aimed, num_segments=slot_count)  38.9 us
    reshape x8, local copies, waits for them, and re-layouts, advance(): products = products.reshape(group_size * per_block, BS * BS)  38.1 us
    gather x8, local copies, waits for them, and re-layouts, advance(): right_rows = rights[chosen].reshape(group_size, per_block, BS, BS)  37.2 us
  transfers between devices with their start and end apart: 2, of which 2 were waited for; matrix products, arithmetic and copies ran while one was open for 0% of the time, Pallas kernels for 0%

commit v1 on v0

v1 whole, which is shorter than its diff:
```python
import jax
import jax.numpy as jnp
from jax import lax
from jax.experimental import pallas as pl
from jax.experimental.pallas import tpu as pltpu
from jax.sharding import Mesh
from jax.sharding import PartitionSpec as P

BS = 64
BLK = BS * BS
OWN_DEV = 2
ROWS = BLK // 128


def low_half(shape):
    return lax.broadcasted_iota(jnp.int32, shape, len(shape) - 1) < BS


def split_rights(right_ref, low_ref, high_ref, spread_ref):
    count = right_ref.shape[0]
    mask8 = low_half((8, 128))

    def unfold(group, carry):
        base = pl.multiple_of(group * 8, 8)
        for m in range(ROWS):
            x = right_ref[pl.ds(base, 8), m * 128 : (m + 1) * 128]
            turned = pltpu.roll(x, BS, 1)
            spread_ref[pl.ds(base * BS + 2 * m, 8, stride=BS), :] = jnp.where(mask8, x, turned)
            spread_ref[pl.ds(base * BS + 2 * m + 1, 8, stride=BS), :] = jnp.where(mask8, turned, x)
        return carry

    lax.fori_loop(0, count // 8, unfold, 0)
    mask = low_half((BS, 128))

    def cut(block, carry):
        x = spread_ref[pl.ds(pl.multiple_of(block * BS, BS), BS), :]
        coarse = x.astype(jnp.bfloat16).astype(jnp.float32)
        fine = x - coarse
        both = jnp.concatenate([coarse, fine], axis=0)
        m2 = jnp.concatenate([mask, mask], axis=0)
        low_ref[block] = jnp.where(m2, both, 0.0).astype(jnp.bfloat16)
        high_ref[block] = jnp.where(m2, 0.0, both).astype(jnp.bfloat16)
        return carry

    lax.fori_loop(0, count, cut, 0, unroll=2)


def prepare(rights):
    count = rights.shape[0]
    half = jax.ShapeDtypeStruct((count, 2 * BS, 128), jnp.bfloat16)
    return pl.pallas_call(
        split_rights,
        out_shape=(half, half),
        scratch_shapes=[pltpu.VMEM((count * BS, 128), jnp.float32)],
        compiler_params=pltpu.CompilerParams(vmem_limit_bytes=32 * 1024 * 1024),
        cost_estimate=pl.CostEstimate(flops=8 * count * BLK, bytes_accessed=12 * count * BLK, transcendentals=0),
        name="split_rights",
    )(rights)


def multiply(
    core_ref, pick_ref, slot_ref, left_ref, low_ref, high_ref, mine_ref, other_ref, flat_ref, acc0, acc1, acc2, acc3, nat_ref
):
    count = left_ref.shape[0]
    per_block = pick_ref.shape[0] // count
    slot_count = acc0.shape[0]
    accs = (acc0, acc1, acc2, acc3)

    def clear(s, carry):
        for acc in accs:
            acc[s] = jnp.zeros(acc.shape[1:], jnp.float32)
        return carry

    lax.fori_loop(0, slot_count, clear, 0)

    def unfold(group, carry):
        base = pl.multiple_of(group * 8, 8)
        for m in range(ROWS):
            flat_ref[pl.ds(base * ROWS + m, 8, stride=ROWS), :] = left_ref[pl.ds(base, 8), m * 128 : (m + 1) * 128]
        return carry

    lax.fori_loop(0, count // 8, unfold, 0)
    mask = low_half((ROWS, 128))

    def one_block(k, carry):
        x = flat_ref[pl.ds(pl.multiple_of(k * ROWS, ROWS), ROWS), :]
        coarse = x.astype(jnp.bfloat16).astype(jnp.float32)
        fine = x - coarse
        even = jnp.where(mask, coarse, pltpu.roll(fine, BS, 1))
        odd = jnp.where(mask, pltpu.roll(coarse, BS, 1), fine)
        tall = jnp.concatenate([even, odd], axis=0).astype(jnp.bfloat16)
        lhs = jnp.concatenate([tall, tall], axis=1)
        first = k * per_block
        for quad in range(per_block // 4):
            pairs = []
            for pair in range(2):
                t = first + quad * 4 + pair * 2
                pairs.append(low_ref[pick_ref[t]] + high_ref[pick_ref[t + 1]])
            both = jnp.concatenate(pairs, axis=1)
            rhs = jnp.concatenate([both[:BS], both[:BS], both[BS:], both[BS:]], axis=0)
            out = jnp.dot(lhs, rhs, preferred_element_type=jnp.float32)
            for pair in range(2):
                t = first + quad * 4 + pair * 2
                part = out[:, pair * 128 : (pair + 1) * 128]
                accs[2 * pair][slot_ref[t]] += part
                accs[2 * pair + 1][slot_ref[t + 1]] += part
        return carry

    lax.fori_loop(0, count, one_block, 0, unroll=8)

    def fold(s, carry):
        low = acc0[s] + acc2[s]
        high = acc1[s] + acc3[s]
        even = low[:ROWS] + pltpu.roll(high[:ROWS], BS, 1)
        odd = pltpu.roll(low[ROWS:], BS, 1) + high[ROWS:]
        nat_ref[pl.ds(pl.multiple_of(s * ROWS, ROWS), ROWS), :] = jnp.where(mask, even, odd)
        return carry

    lax.fori_loop(0, slot_count, fold, 0, unroll=8)

    pieces = mine_ref.shape[0]
    tiles = ROWS // (2 * pieces)
    core = core_ref[0]

    def place(group, carry):
        base = pl.multiple_of(group * 8, 8)
        for out_ref, half in ((mine_ref, core), (other_ref, 1 - core)):
            first = base * ROWS + half * (ROWS // 2)
            for m in range(ROWS // 2):
                out_ref[m // tiles, pl.ds(base, 8), (m % tiles) * 128 : (m % tiles + 1) * 128] = nat_ref[
                    pl.ds(first + m, 8, stride=ROWS), :
                ]
        return carry

    lax.fori_loop(0, slot_count // 8, place, 0)


def products(core, picks, targets, panel, low, high, slot_count, pieces):
    smem = pl.BlockSpec(memory_space=pltpu.SMEM)
    vmem = pl.BlockSpec(memory_space=pltpu.VMEM)
    acc = pltpu.VMEM((slot_count, BS, 128), jnp.float32)
    out = jax.ShapeDtypeStruct((pieces, slot_count, BLK // (2 * pieces)), jnp.float32)
    flops = 2 * picks.shape[0] * BS * BS * BS * 4
    return pl.pallas_call(
        multiply,
        out_shape=(out, out),
        in_specs=[smem, smem, smem, vmem, vmem, vmem],
        out_specs=(vmem, vmem),
        scratch_shapes=[
            pltpu.VMEM((panel.shape[0] * ROWS, 128), jnp.float32),
            acc,
            acc,
            acc,
            acc,
            pltpu.VMEM((slot_count * ROWS, 128), jnp.float32),
        ],
        compiler_params=pltpu.CompilerParams(vmem_limit_bytes=48 * 1024 * 1024),
        cost_estimate=pl.CostEstimate(flops=flops, bytes_accessed=8 * 1024 * 1024, transcendentals=0),
        name="multiply",
    )(core, picks, targets, panel, low, high)


def local(left_blocks, right_blocks, task_right, task_slot, recv_owner):
    row_count = lax.axis_size("row")
    chips = lax.axis_size("y")
    group = ("y", "core")
    members = 2 * chips
    slot_count = recv_owner.shape[1]
    capacity = slot_count // row_count
    core = lax.axis_index("core").astype(jnp.int32).reshape(1)

    panel = lax.all_gather(left_blocks[0], group, axis=0, tiled=True)
    low, high = prepare(right_blocks[0, 0])
    mine, other = products(core, task_right[0, 0], task_slot[0, 0], panel, low, high, slot_count, chips)
    mine = mine + lax.ppermute(other, "core", [(0, 1), (1, 0)])
    pieces = lax.all_to_all(mine, "y", split_axis=0, concat_axis=0, tiled=True)
    width = pieces.shape[2]
    piece = pieces.sum(axis=0).reshape(row_count, capacity, width)
    received = lax.all_to_all(piece, "row", split_axis=0, concat_axis=0, tiled=True).reshape(slot_count, width)
    owners = recv_owner[0]
    owned_ids = jnp.arange(OWN_DEV * members, dtype=jnp.int32)
    selector = (owners[None, :] == owned_ids[:, None]).astype(jnp.float32)
    owned = jnp.dot(selector, received, precision=lax.Precision.HIGHEST, preferred_element_type=jnp.float32)
    own = lax.all_to_all(
        owned.reshape(members, OWN_DEV, width), group, split_axis=0, concat_axis=0, tiled=True
    )
    own = own.reshape(chips, 2, OWN_DEV, width).transpose(2, 1, 0, 3)
    return own.reshape(1, OWN_DEV, BLK)


def solution(mesh):
    fine = Mesh(mesh.devices.reshape(mesh.shape["row"], mesh.shape["rep"] // 2, 2), ("row", "y", "core"))
    group = ("y", "core")
    in_specs = (
        P("row", group, None),
        P("row", group, None, None),
        P("row", group, None),
        P("row", group, None),
        P("row", None),
    )
    out_specs = P("row", group, None)
    return jax.shard_map(local, mesh=fine, in_specs=in_specs, out_specs=out_specs, check_vma=False)
```

time: 556 us -> 158 us (0.28)
  local copies, waits for them, and re-layouts: 175 us -> 6.93 us
  waiting for transfers between devices: 169 us -> 64.1 us
  matrix products: 79.9 us -> 0.2 us
  other arithmetic: 45.1 us -> 0.16 us
  blocking collectives: 69 us -> 40.1 us
  Pallas kernels: 0 us -> 18 us
  starting transfers between devices: 0.04 us -> 15 us
    unnamed x3 -> x1, waiting for transfers between devices: 114 us -> 0.71 us
    dot_general x9 -> x1, matrix products: 79.9 us -> 0.2 us  [local(): jnp.dot(selector, received, precision=lax.Precision.HIGHEST, preferred_el...]
    reshape x26 -> x3, local copies, waits for them, and re-layouts: 78.6 us -> 1.4 us  [the longest x1 0.69 us: local(): piece = pieces.sum(axis=0).reshape(row_count, capacity, width)]
    transpose x8 -> x1, local copies, waits for them, and re-layouts: 42.7 us -> 0.01 us  [local(): own = own.reshape(chips, 2, OWN_DEV, width).transpose(2, 1, 0, 3)]
    scatter-add x8 -> x0, other arithmetic: 38.9 us -> none  [advance(): jax.ops.segment_sum(products, aimed, num_segments=slot_count)]
    gather x8 -> x0, local copies, waits for them, and re-layouts: 37.2 us -> none  [advance(): right_rows = rights[chosen].reshape(group_size, per_block, BS, BS)]
    all_to_all x1 -> x2, blocking collectives: 69 us -> 40.1 us  [the longest x1 27.3 us: local(): pieces = lax.all_to_all(mine, 'y', split_axis=0, concat_axis=0, tiled=True)]
    pallas_call x0 -> x2, Pallas kernels: none -> 18 us  [the longest x1 15.6 us: products(): pl.pallas_call(multiply, out_shape=(out, out), in_specs=[smem, smem, smem...]
  transfers between devices with their start and end apart: 2 -> 3, of which waited for: 2 -> 3; matrix products, arithmetic and copies ran while one was open for 0% -> 0% of each run, Pallas kernels for 0% -> 2%
where the time goes in v1:
time: 158 us
  waiting for transfers between devices  64.1 us (41%)
  blocking collectives  40.1 us (25%)
  Pallas kernels  18 us (11%)
  starting transfers between devices  15 us (9%)
  between operations  13.5 us (9%)
  local copies, waits for them, and re-layouts  6.93 us (4%)
    all_gather x1, waiting for transfers between devices, local(): panel = lax.all_gather(left_blocks[0], group, axis=0, tiled=True)  50 us
    all_to_all x1, blocking collectives, local(): pieces = lax.all_to_all(mine, 'y', split_axis=0, concat_axis=0, tiled=True)  27.3 us
    pallas_call x1, Pallas kernels, products(): pl.pallas_call(multiply, out_shape=(out, out), in_specs=[smem, smem, smem...  15.6 us
    all_to_all x1, starting transfers between devices, local(): lax.all_to_all(piece, 'row', split_axis=0, concat_axis=0, tiled=True)  12.8 us
    all_to_all x1, blocking collectives, local(): lax.all_to_all(owned.reshape(members, OWN_DEV, width), group, split_axis=...  12.8 us
    all_to_all x1, waiting for transfers between devices, local(): lax.all_to_all(piece, 'row', split_axis=0, concat_axis=0, tiled=True)  11.4 us
    unnamed x12, local copies, waits for them, and re-layouts  5.5 us
  transfers between devices with their start and end apart: 3, of which 3 were waited for; matrix products, arithmetic and copies ran while one was open for 0% of the time, Pallas kernels for 2%

profile of v1, /device:TPU:1, one launch (start us, length us, event | category | flops | bytes accessed | tf_op | source)
XLA Modules:
  0.0 158.0 jit_solution(7624832614073309985)
XLA Ops:
  6.5 0.0 all-gather.3.cloned.1.call-start
  6.5 0.7 all-gather.3.cloned.1.call-update
  7.3 0.0 copy-start
  7.3 1.2 copy-done
  8.5 2.4 %split_rights.1 = (bf16[64,128,128]{2,1,0:T(8,128)(2,1)S(1)}, bf16[64,128,128]{2,1,0:T(8,128)(2,1)S(1)}) custom-call(f32[64,4096]{1,0:T(8,128)S(1)} %bitcast.12), custom_call_target="tpu_custom_call" | custom-call | flops 2097152 | bytes 3145728 | tf_op jit(solution)/shard_map/split_rights/pallas_call | solution.py:51
  10.9 0.0 copy-start.2
  10.9 1.3 copy-done.2
  12.2 50.0 %all-gather.3.cloned.1.call-done = f32[1,128,4096]{2,1,0:T(8,128)} async-done(((f32[1,8,4096]{2,1,0:T(8,128)}), f32[1,128,4096]{2,1,0:T(8,128)}) %all-gather.3.cloned.1.call-update) | async-done | bytes 2097168 | tf_op jit(solution)/shard_map/all_gather | solution.py:172
  62.3 0.0 copy-start.1
  62.3 1.6 %copy-done.1 = f32[1,128,4096]{2,1,0:T(8,128)S(1)} copy-done((f32[1,128,4096]{2,1,0:T(8,128)S(1)}, f32[1,128,4096]{2,1,0:T(8,128)}, u32[]{:S(2)}) %copy-start.1) | copy-done | bytes 2097176
  63.8 0.0 copy-start.3
  63.8 0.7 copy-done.3
  64.5 0.0 copy-start.4
  64.5 0.7 copy-done.4
  65.2 15.6 %multiply.5 = (f32[8,96,256]{2,1,0:T(8,128)S(1)}, f32[8,96,256]{2,1,0:T(8,128)S(1)}) custom-call(s32[1]{0:T(128)} %bitcast.1.core_ref, s32[1024]{0:T(1024)S(1)} %bitcast.14, s32[1024]{0:T(1024)S(1)} %bitcast.15, f32[128,4096]{1,0:T(8,128)S(1)} %bitcast.13, bf16[64,128,128]{2,1,0:T(8,128)(2,1)S(1)} %get-tuple-element.9.low_ref, bf16[64,128,128]{2,1,0:T(8,128)(2,1)} %copy-done.2), custom_call_target="tpu_custom_call" | custom-call | flops 2147483648 | bytes 8388608 | tf_op jit(solution)/shard_map/multiply/pallas_call | solution.py:144
  80.8 2.2 %collective-permute-start = (f32[8,96,256]{2,1,0:T(8,128)S(1)}, f32[8,96,256]{2,1,0:T(8,128)S(1)}, u32[]{:S(2)}, u32[]{:S(2)}) collective-permute-start(f32[8,96,256]{2,1,0:T(8,128)S(1)} %get-tuple-element.12), channel_id=1, source_target_pairs={{0,1},{1,0},{2,3},{3,2},{4,5},{5,4},{6,7},{7,6},{8,9},{9,8},{10,11... | collective-permute-start | bytes 2359304 | tf_op jit(solution)/shard_map/ppermute | solution.py:175
  83.0 2.0 %collective-permute-done = f32[8,96,256]{2,1,0:T(8,128)S(1)} collective-permute-done((f32[8,96,256]{2,1,0:T(8,128)S(1)}, f32[8,96,256]{2,1,0:T(8,128)S(1)}, u32[]{:S(2)}, u32[]{:S(2)}) %collective-permute-start) | collective-permute-done | bytes 786464 | tf_op jit(solution)/shard_map/ppermute | solution.py:175
  85.0 0.1 add.7
  85.1 0.0 copy-start.5
  85.1 27.3 %all_to_all.15 = f32[8,96,256]{2,1,0:T(8,128)S(1)} all-to-all(f32[8,96,256]{2,1,0:T(8,128)S(1)} %add.7), channel_id=1, replica_groups=mesh['row'=48,'y'=8,'core'=2] {'y'}, dimensions={0} | all-to-all | bytes 1572864 | tf_op jit(solution)/shard_map/all_to_all | solution.py:176
  112.5 0.1 reduce_sum.9
  112.5 0.7 reshape.35
  113.2 12.8 %all-to-all-start.1 = ((f32[48,2,256]{2,1,0:T(2,128)}), f32[48,2,256]{2,1,0:T(2,128)S(1)}, u32[]{:S(2)}, u32[]{:S(2)}) async-start(f32[48,2,256]{2,1,0:T(2,128)} %reshape.35), calls=%async_computation.1 | async-start | bytes 196608 | tf_op jit(solution)/shard_map/all_to_all | solution.py:179
  126.0 11.4 %all-to-all-done.1 = f32[48,2,256]{2,1,0:T(2,128)S(1)} async-done(((f32[48,2,256]{2,1,0:T(2,128)}), f32[48,2,256]{2,1,0:T(2,128)S(1)}, u32[]{:S(2)}, u32[]{:S(2)}) %all-to-all-start.1) | async-done | bytes 98336 | tf_op jit(solution)/shard_map/all_to_all | solution.py:179
  137.4 0.1 reshape.40
  137.4 0.0 copy-done.5
  137.5 0.2 fusion
  137.7 12.8 %all_to_all.16 = f32[16,2,256]{2,1,0:T(2,128)S(1)} all-to-all(f32[16,2,256]{2,1,0:T(2,128)S(1)} %copy.7), channel_id=1, replica_groups=mesh['row'=48,'y'=8,'core'=2] {'y','core'}, dimensions={0} | all-to-all | bytes 65536 | tf_op jit(solution)/shard_map/all_to_all | solution.py:184
  150.5 0.6 reshape.38
  (3 shorter events, 0.0 us)
Async XLA Ops:
  6.5 55.7 %all-gather.3.cloned.1.call-start = ((), (), s32[]{:S(2)}) async-start(), calls=%async_computation.3 | async-start | bytes 2228224 | tf_op jit(solution)/shard_map/all_gather | solution.py:172
  7.3 1.2 copy-start
  10.9 1.3 copy-start.2
  62.3 1.6 %copy-start.1 = (f32[1,128,4096]{2,1,0:T(8,128)S(1)}, f32[1,128,4096]{2,1,0:T(8,128)}, u32[]{:S(2)}) copy-start(f32[1,128,4096]{2,1,0:T(8,128)} %all-gather.3.cloned.1.call-done) | copy-start | bytes 6291460
  63.8 0.7 copy-start.3
  64.5 0.7 copy-start.4
  80.8 4.2 %collective-permute-start = (f32[8,96,256]{2,1,0:T(8,128)S(1)}, f32[8,96,256]{2,1,0:T(8,128)S(1)}, u32[]{:S(2)}, u32[]{:S(2)}) collective-permute-start(f32[8,96,256]{2,1,0:T(8,128)S(1)} %get-tuple-element.12), channel_id=1, source_target_pairs={{0,1},{1,0},{2,3},{3,2},{4,5},{5,4},{6,7},{7,6},{8,9},{9,8},{10,11... | collective-permute-start | bytes 2359304 | tf_op jit(solution)/shard_map/ppermute | solution.py:175
  85.1 52.3 %copy-start.5 = (s32[1,96]{1,0:T(1,128)S(1)}, s32[1,96]{1,0:T(1,128)}, u32[]{:S(2)}) copy-start(s32[1,96]{1,0:T(1,128)} %param.9) | copy-start | bytes 1156
  113.2 24.2 %all-to-all-start.1 = ((f32[48,2,256]{2,1,0:T(2,128)}), f32[48,2,256]{2,1,0:T(2,128)S(1)}, u32[]{:S(2)}, u32[]{:S(2)}) async-start(f32[48,2,256]{2,1,0:T(2,128)} %reshape.35), calls=%async_computation.1 | async-start | bytes 196608 | tf_op jit(solution)/shard_map/all_to_all | solution.py:179
Sparse Core Ops, SparseCore 0:
  9.8 52.4 all-gather.2

commit v2 on v1

v2 whole, which is shorter than its diff:
```python
import jax
import jax.numpy as jnp
from jax import lax
from jax.experimental import pallas as pl
from jax.experimental.pallas import tpu as pltpu
from jax.sharding import Mesh
from jax.sharding import PartitionSpec as P

BS = 64
BLK = BS * BS
OWN_DEV = 2
ROWS = BLK // 128
SWAP = [(0, 1), (1, 0)]


def low_half(shape):
    return lax.broadcasted_iota(jnp.int32, shape, len(shape) - 1) < BS


def split_rights(right_ref, parts_ref, spread_ref):
    count = right_ref.shape[0]
    mask = low_half((8, 128))

    def unfold(group, carry):
        base = pl.multiple_of(group * 8, 8)
        for m in range(ROWS):
            x = right_ref[pl.ds(base, 8), m * 128 : (m + 1) * 128]
            turned = pltpu.roll(x, BS, 1)
            spread_ref[pl.ds(base * BS + 2 * m, 8, stride=BS), :] = jnp.where(mask, x, turned)
            spread_ref[pl.ds(base * BS + 2 * m + 1, 8, stride=BS), :] = jnp.where(mask, turned, x)
        return carry

    lax.fori_loop(0, count // 8, unfold, 0)

    def cut(block, carry):
        x = spread_ref[pl.ds(pl.multiple_of(block * BS, BS), BS), :]
        coarse = x.astype(jnp.bfloat16)
        parts_ref[block, :BS, :] = coarse
        parts_ref[block, BS:, :] = (x - coarse.astype(jnp.float32)).astype(jnp.bfloat16)
        return carry

    lax.fori_loop(0, count, cut, 0, unroll=4)


def prepare(rights):
    count = rights.shape[0]
    return pl.pallas_call(
        split_rights,
        out_shape=jax.ShapeDtypeStruct((count, 2 * BS, 128), jnp.bfloat16),
        scratch_shapes=[pltpu.VMEM((count * BS, 128), jnp.float32)],
        compiler_params=pltpu.CompilerParams(vmem_limit_bytes=16 * 1024 * 1024),
        cost_estimate=pl.CostEstimate(flops=8 * count * BLK, bytes_accessed=12 * count * BLK, transcendentals=0),
        name="split_rights",
    )(rights)


def multiply(
    core_ref, own_tasks_ref, twin_tasks_ref, left_ref, own_ref, twin_ref, mine_ref, other_ref,
    flat_ref, acc0, acc1, acc2, acc3, nat_ref,
):
    chips, share = left_ref.shape[0], left_ref.shape[1]
    count = chips * share
    per_block = own_tasks_ref.shape[1] // (2 * count)
    slot_count = acc0.shape[0]
    accs = (acc0, acc1, acc2, acc3)
    core = core_ref[0]

    def clear(s, carry):
        for acc in accs:
            acc[s] = jnp.zeros(acc.shape[1:], jnp.float32)
        return carry

    lax.fori_loop(0, slot_count, clear, 0, unroll=4)

    def unfold(chip, carry):
        for m in range(ROWS):
            flat_ref[pl.ds(chip * share * ROWS + m, share, stride=ROWS), :] = left_ref[chip, :, m * 128 : (m + 1) * 128]
        return carry

    lax.fori_loop(0, chips, unfold, 0)
    mask = low_half((ROWS, 128))
    wide = low_half((2 * BS, 128))

    def one_block(k, carry):
        x = flat_ref[pl.ds(pl.multiple_of(k * ROWS, ROWS), ROWS), :]
        coarse = x.astype(jnp.bfloat16).astype(jnp.float32)
        fine = x - coarse
        even = jnp.where(mask, coarse, pltpu.roll(fine, BS, 1))
        odd = jnp.where(mask, pltpu.roll(coarse, BS, 1), fine)
        tall = jnp.concatenate([even, odd], axis=0).astype(jnp.bfloat16)
        lhs = jnp.concatenate([tall, tall], axis=1)
        first = ((k // share) * 2 * share + core * share + k % share) * per_block
        for tasks_ref, parts_ref in ((own_tasks_ref, own_ref), (twin_tasks_ref, twin_ref)):
            for quad in range(per_block // 4):
                pairs = []
                for pair in range(2):
                    t = first + quad * 4 + pair * 2
                    pairs.append(jnp.where(wide, parts_ref[tasks_ref[0, t]], parts_ref[tasks_ref[0, t + 1]]))
                both = jnp.concatenate(pairs, axis=1)
                rhs = jnp.concatenate([both[:BS], both[:BS], both[BS:], both[BS:]], axis=0)
                out = jnp.dot(lhs, rhs, preferred_element_type=jnp.float32)
                for pair in range(2):
                    t = first + quad * 4 + pair * 2
                    part = out[:, pair * 128 : (pair + 1) * 128]
                    accs[2 * pair][tasks_ref[1, t]] += part
                    accs[2 * pair + 1][tasks_ref[1, t + 1]] += part
        return carry

    lax.fori_loop(0, count, one_block, 0, unroll=8)

    def fold(s, carry):
        low = acc0[s] + acc2[s]
        high = acc1[s] + acc3[s]
        even = low[:ROWS] + pltpu.roll(high[:ROWS], BS, 1)
        odd = pltpu.roll(low[ROWS:], BS, 1) + high[ROWS:]
        nat_ref[pl.ds(pl.multiple_of(s * ROWS, ROWS), ROWS), :] = jnp.where(mask, even, odd)
        return carry

    lax.fori_loop(0, slot_count, fold, 0, unroll=8)

    tiles = ROWS // (2 * mine_ref.shape[0])

    def place(group, carry):
        base = pl.multiple_of(group * 8, 8)
        for out_ref, half in ((mine_ref, core), (other_ref, 1 - core)):
            first = base * ROWS + half * (ROWS // 2)
            for m in range(ROWS // 2):
                out_ref[m // tiles, pl.ds(base, 8), (m % tiles) * 128 : (m % tiles + 1) * 128] = nat_ref[
                    pl.ds(first + m, 8, stride=ROWS), :
                ]
        return carry

    lax.fori_loop(0, slot_count // 8, place, 0)


def products(core, own_tasks, twin_tasks, panel, own, twin, slot_count):
    chips, share, _ = panel.shape
    smem = pl.BlockSpec(memory_space=pltpu.SMEM)
    vmem = pl.BlockSpec(memory_space=pltpu.VMEM)
    acc = pltpu.VMEM((slot_count, BS, 128), jnp.float32)
    out = jax.ShapeDtypeStruct((chips, slot_count, BLK // (2 * chips)), jnp.float32)
    flops = 2 * own_tasks.shape[1] * BS * BS * BS * 4
    return pl.pallas_call(
        multiply,
        out_shape=(out, out),
        in_specs=[smem, smem, smem, vmem, vmem, vmem],
        out_specs=(vmem, vmem),
        scratch_shapes=[
            pltpu.VMEM((chips * share * ROWS, 128), jnp.float32),
            acc,
            acc,
            acc,
            acc,
            pltpu.VMEM((slot_count * ROWS, 128), jnp.float32),
        ],
        compiler_params=pltpu.CompilerParams(vmem_limit_bytes=32 * 1024 * 1024),
        cost_estimate=pl.CostEstimate(flops=flops, bytes_accessed=8 * 1024 * 1024, transcendentals=0),
        name="multiply",
    )(core, own_tasks, twin_tasks, panel, own, twin)


def exchange(x, axis):
    return lax.all_to_all(x, axis, split_axis=0, concat_axis=0, tiled=True)


def local(left_blocks, right_blocks, task_right, task_slot, recv_owner):
    row_count = lax.axis_size("row")
    chips = lax.axis_size("y")
    group = ("y", "core")
    members = 2 * chips
    slot_count = recv_owner.shape[1]
    capacity = slot_count // row_count
    core = lax.axis_index("core").astype(jnp.int32).reshape(1)

    panel = exchange(jnp.broadcast_to(left_blocks, (chips,) + left_blocks.shape[1:]), "y")
    rights = right_blocks[0, 0]
    tasks = jnp.concatenate([task_right[0], task_slot[0]], axis=0)
    twin_rights = lax.ppermute(rights, "core", SWAP)
    twin_tasks = lax.ppermute(tasks, "core", SWAP)
    own = prepare(rights)
    twin = prepare(twin_rights)
    mine, other = products(core, tasks, twin_tasks, panel, own, twin, slot_count)
    mine = mine + lax.ppermute(other, "core", SWAP)
    pieces = exchange(mine, "y")
    width = pieces.shape[2]
    piece = pieces.sum(axis=0).reshape(row_count, capacity, width)
    received = exchange(piece, "row").reshape(slot_count, width)
    owners = recv_owner[0]
    owned_ids = jnp.arange(OWN_DEV * members, dtype=jnp.int32)
    selector = (owners[None, :] == owned_ids[:, None]).astype(jnp.float32)
    owned = jnp.dot(selector, received, precision=lax.Precision.HIGHEST, preferred_element_type=jnp.float32)
    own_blocks = exchange(owned.reshape(members, OWN_DEV, width), group)
    own_blocks = own_blocks.reshape(chips, 2, OWN_DEV, width).transpose(2, 1, 0, 3)
    return own_blocks.reshape(1, OWN_DEV, BLK)


def solution(mesh):
    fine = Mesh(mesh.devices.reshape(mesh.shape["row"], mesh.shape["rep"] // 2, 2), ("row", "y", "core"))
    group = ("y", "core")
    in_specs = (
        P("row", group, None),
        P("row", group, None, None),
        P("row", group, None),
        P("row", group, None),
        P("row", None),
    )
    out_specs = P("row", group, None)
    return jax.shard_map(local, mesh=fine, in_specs=in_specs, out_specs=out_specs, check_vma=False)
```

time: 158 us -> 128 us (0.81)
  waiting for transfers between devices: 64.1 us -> 20 us
  starting transfers between devices: 15 us -> 44.1 us
  between operations: 13.5 us -> 0.16 us
  blocking collectives: 40.1 us -> 38.3 us
    all_gather x1 -> x0, waiting for transfers between devices: 50 us -> none  [local(): panel = lax.all_gather(left_blocks[0], group, axis=0, tiled=True)]
    ppermute x1 -> x3, starting transfers between devices: 2.17 us -> 18.5 us  [the longest x1 9.03 us: local(): twin_rights = lax.ppermute(rights, 'core', SWAP)]
    all_to_all x1 -> x2, starting transfers between devices: 12.8 us -> 25.6 us  [exchange(): return lax.all_to_all(x, axis, split_axis=0, concat_axis=0, tiled=True)]
    all_to_all x1 -> x2, waiting for transfers between devices: 11.4 us -> 18.1 us  [exchange(): return lax.all_to_all(x, axis, split_axis=0, concat_axis=0, tiled=True)]
    pallas_call x1 -> x2, Pallas kernels: 2.39 us -> 5.15 us  [prepare(): pl.pallas_call(split_rights, out_shape=jax.ShapeDtypeStruct((count, 2 * B...]
    unnamed x12, local copies, waits for them, and re-layouts: 5.5 us -> 2.93 us
    pallas_call x1, Pallas kernels: 15.6 us -> 13.5 us  [products(): pl.pallas_call(multiply, out_shape=(out, out), in_specs=[smem, smem, smem...]
    broadcast_in_dim x0 -> x1, local copies, waits for them, and re-layouts: none -> 2.06 us  [local(): jnp.broadcast_to(left_blocks, (chips,) + left_blocks.shape[1:])]
  transfers between devices with their start and end apart: 3 -> 5, of which waited for: 3 -> 3; matrix products, arithmetic and copies ran while one was open for 0% -> 0% of each run, Pallas kernels for 2% -> 4%
where the time goes in v2:
time: 128 us
  starting transfers between devices  44.1 us (34%)
  blocking collectives  38.3 us (30%)
  waiting for transfers between devices  20 us (16%)
  Pallas kernels  18.6 us (15%)
  local copies, waits for them, and re-layouts  6.43 us (5%)
    all_to_all x2, blocking collectives, exchange(): return lax.all_to_all(x, axis, split_axis=0, concat_axis=0, tiled=True)  38.3 us
    all_to_all x2, starting transfers between devices, exchange(): return lax.all_to_all(x, axis, split_axis=0, concat_axis=0, tiled=True)  25.6 us
    all_to_all x2, waiting for transfers between devices, exchange(): return lax.all_to_all(x, axis, split_axis=0, concat_axis=0, tiled=True)  18.1 us
    pallas_call x1, Pallas kernels, products(): pl.pallas_call(multiply, out_shape=(out, out), in_specs=[smem, smem, smem...  13.5 us
    ppermute x1, starting transfers between devices, local(): twin_rights = lax.ppermute(rights, 'core', SWAP)  9.03 us
    ppermute x1, starting transfers between devices, local(): mine = mine + lax.ppermute(other, 'core', SWAP)  7.51 us
    pallas_call x2, Pallas kernels, prepare(): pl.pallas_call(split_rights, out_shape=jax.ShapeDtypeStruct((count, 2 * B...  5.15 us
    unnamed x12, local copies, waits for them, and re-layouts  2.93 us
  transfers between devices with their start and end apart: 5, of which 3 were waited for; matrix products, arithmetic and copies ran while one was open for 0% of the time, Pallas kernels for 4%

profile of v2, /device:TPU:1, one launch (start us, length us, event | category | flops | bytes accessed | tf_op | source)
XLA Modules:
  0.0 128.0 jit_solution(17367079544967526070)
XLA Ops:
  0.0 0.0 copy-start.2
  0.0 0.0 copy-start.4
  0.0 2.1 %broadcast_in_dim.9 = f32[8,8,4096]{2,1,0:T(8,128)} broadcast(f32[8,4096]{1,0:T(8,128)} %bitcast.14), dimensions={1,2} | broadcast | bytes 1179648 | tf_op jit(solution)/shard_map/broadcast_in_dim | solution.py:175
  2.1 7.7 %all-to-all-start = ((f32[8,8,4096]{2,1,0:T(8,128)}), f32[8,8,4096]{2,1,0:T(8,128)}, u32[]{:S(2)}, u32[]{:S(2)}) async-start(f32[8,8,4096]{2,1,0:T(8,128)} %broadcast_in_dim.9), calls=%async_computation | async-start | bytes 2097152 | tf_op jit(solution)/shard_map/all_to_all | solution.py:163
  9.7 0.0 copy-done.2
  9.7 9.0 %collective-permute-start.1 = (f32[64,4096]{1,0:T(8,128)S(1)}, f32[64,4096]{1,0:T(8,128)}, u32[]{:S(2)}, u32[]{:S(2)}) collective-permute-start(f32[64,4096]{1,0:T(8,128)S(1)} %bitcast.12), channel_id=1, source_target_pairs={{0,1},{1,0},{2,3},{3,2},{4,5},{5,4},{6,7},{7,6},{8,9},{9,8},{10,11... | collective-permute-start | bytes 3145736 | tf_op jit(solution)/shard_map/ppermute | solution.py:178
  18.8 0.0 copy-done.4
  18.8 0.0 copy-done.3
  18.8 1.9 %collective-permute-start = (s32[2,1024]{1,0:T(2,128)S(1)}, s32[2,1024]{1,0:T(2,128)S(1)}, u32[]{:S(2)}, u32[]{:S(2)}) collective-permute-start(s32[2,1024]{1,0:T(2,128)S(1)} %pad_add_fusion.own_tasks_ref), channel_id=1, source_target_pairs={{0,1},{1,0},{2,3},{3,2},{4,5},{5,4},{6,7},{7,6},{8,9},{9,8},{10,11... | collective-permute-start | bytes 24584 | tf_op jit(solution)/shard_map/ppermute | solution.py:179
  20.7 2.0 %split_rights.2.own_ref = bf16[64,128,128]{2,1,0:T(8,128)(2,1)S(1)} custom-call(f32[64,4096]{1,0:T(8,128)S(1)} %bitcast.13), custom_call_target="tpu_custom_call" | custom-call | flops 2097152 | bytes 3145728 | tf_op jit(solution)/shard_map/split_rights/pallas_call | solution.py:47
  22.7 0.0 collective-permute-done.1.right_ref
  22.7 3.2 %split_rights.3.twin_ref = bf16[64,128,128]{2,1,0:T(8,128)(2,1)S(1)} custom-call(f32[64,4096]{1,0:T(8,128)} %collective-permute-done.1.right_ref), custom_call_target="tpu_custom_call" | custom-call | flops 2097152 | bytes 3145728 | tf_op jit(solution)/shard_map/split_rights/pallas_call | solution.py:47
  25.9 0.0 copy-start
  25.9 1.3 %copy-done = bf16[64,128,128]{2,1,0:T(8,128)(2,1)} copy-done((bf16[64,128,128]{2,1,0:T(8,128)(2,1)}, bf16[64,128,128]{2,1,0:T(8,128)(2,1)S(1)}, u32[]{:S(2)}) %copy-start) | copy-done | bytes 2097176
  27.2 0.0 collective-permute-done.twin_tasks_ref
  27.2 6.7 %all-to-all-done.left_ref = f32[8,8,4096]{2,1,0:T(8,128)} async-done(((f32[8,8,4096]{2,1,0:T(8,128)}), f32[8,8,4096]{2,1,0:T(8,128)}, u32[]{:S(2)}, u32[]{:S(2)}) %all-to-all-start) | async-done | bytes 1048608 | tf_op jit(solution)/shard_map/all_to_all | solution.py:163
  34.0 1.6 %copy-done.1 = bf16[64,128,128]{2,1,0:T(8,128)(2,1)S(1)} copy-done((bf16[64,128,128]{2,1,0:T(8,128)(2,1)S(1)}, bf16[64,128,128]{2,1,0:T(8,128)(2,1)}, u32[]{:S(2)}) %copy-start.1) | copy-done | bytes 2097176
  35.5 13.5 %multiply.5 = (f32[8,96,256]{2,1,0:T(8,128)S(1)}, f32[8,96,256]{2,1,0:T(8,128)S(1)}) custom-call(s32[1]{0:T(128)} %bitcast.1.core_ref, s32[2,1024]{1,0:T(2,128)S(1)} %pad_add_fusion.own_tasks_ref, s32[2,1024]{1,0:T(2,128)S(1)} %collective-permute-done.twin_tasks_ref, f32[8,8,4096]{2,1,0:T(8,128)} %all-to-all-done.left_ref, ...), custom_call_target="tpu_custom_call" | custom-call | flops 2147483648 | bytes 8388608 | tf_op jit(solution)/shard_map/multiply/pallas_call | solution.py:143
  49.0 7.5 %collective-permute-start.2 = (f32[8,96,256]{2,1,0:T(8,128)S(1)}, f32[8,96,256]{2,1,0:T(8,128)S(1)}, u32[]{:S(2)}, u32[]{:S(2)}) collective-permute-start(f32[8,96,256]{2,1,0:T(8,128)S(1)} %get-tuple-element.8), channel_id=1, source_target_pairs={{0,1},{1,0},{2,3},{3,2},{4,5},{5,4},{6,7},{7,6},{8,9},{9,8},{10,11... | collective-permute-start | bytes 2359304 | tf_op jit(solution)/shard_map/ppermute | solution.py:183
  56.5 1.9 %collective-permute-done.2 = f32[8,96,256]{2,1,0:T(8,128)S(1)} collective-permute-done((f32[8,96,256]{2,1,0:T(8,128)S(1)}, f32[8,96,256]{2,1,0:T(8,128)S(1)}, u32[]{:S(2)}, u32[]{:S(2)}) %collective-permute-start.2) | collective-permute-done | bytes 786464 | tf_op jit(solution)/shard_map/ppermute | solution.py:183
  58.4 0.1 add.7
  58.5 0.0 copy-start.5
  58.5 26.0 %all_to_all.20 = f32[8,96,256]{2,1,0:T(8,128)S(1)} all-to-all(f32[8,96,256]{2,1,0:T(8,128)S(1)} %add.7), channel_id=1, replica_groups=mesh['row'=48,'y'=8,'core'=2] {'y'}, dimensions={0} | all-to-all | bytes 1572864 | tf_op jit(solution)/shard_map/all_to_all | solution.py:163
  84.5 0.1 reduce_sum.9
  84.6 0.7 reshape.35
  85.3 18.0 %all-to-all-start.2 = ((f32[48,2,256]{2,1,0:T(2,128)}), f32[48,2,256]{2,1,0:T(2,128)S(1)}, u32[]{:S(2)}, u32[]{:S(2)}) async-start(f32[48,2,256]{2,1,0:T(2,128)} %reshape.35), calls=%async_computation.2 | async-start | bytes 196608 | tf_op jit(solution)/shard_map/all_to_all | solution.py:163
  103.3 11.4 %all-to-all-done.2 = f32[48,2,256]{2,1,0:T(2,128)S(1)} async-done(((f32[48,2,256]{2,1,0:T(2,128)}), f32[48,2,256]{2,1,0:T(2,128)S(1)}, u32[]{:S(2)}, u32[]{:S(2)}) %all-to-all-start.2) | async-done | bytes 98336 | tf_op jit(solution)/shard_map/all_to_all | solution.py:163
  114.7 0.1 reshape.39
  114.7 0.0 copy-done.5
  114.7 0.2 fusion
  115.0 12.3 %all_to_all.21 = f32[16,2,256]{2,1,0:T(2,128)S(1)} all-to-all(f32[16,2,256]{2,1,0:T(2,128)S(1)} %copy.7), channel_id=1, replica_groups=mesh['row'=48,'y'=8,'core'=2] {'y','core'}, dimensions={0} | all-to-all | bytes 65536 | tf_op jit(solution)/shard_map/all_to_all | solution.py:163
  127.3 0.6 reshape.38
  (6 shorter events, 0.1 us)
Async XLA Ops:
  0.0 9.7 %copy-start.2 = (f32[1,1,64,4096]{3,2,1,0:T(8,128)S(1)}, f32[1,1,64,4096]{3,2,1,0:T(8,128)}, u32[]{:S(2)}) copy-start(f32[1,1,64,4096]{3,2,1,0:T(8,128)} %param.6) | copy-start | bytes 3145732
  0.0 18.8 %copy-start.4 = (s32[1,1,1024]{2,1,0:T(1,128)S(1)}, s32[1,1,1024]{2,1,0:T(1,128)}, u32[]{:S(2)}) copy-start(s32[1,1,1024]{2,1,0:T(1,128)} %param.7) | copy-start | bytes 12292
  0.0 18.8 %copy-start.3 = (s32[1,1,1024]{2,1,0:T(1,128)S(1)}, s32[1,1,1024]{2,1,0:T(1,128)}, u32[]{:S(2)}) copy-start(s32[1,1,1024]{2,1,0:T(1,128)} %param.8) | copy-start | bytes 12292
  2.1 31.9 %all-to-all-start = ((f32[8,8,4096]{2,1,0:T(8,128)}), f32[8,8,4096]{2,1,0:T(8,128)}, u32[]{:S(2)}, u32[]{:S(2)}) async-start(f32[8,8,4096]{2,1,0:T(8,128)} %broadcast_in_dim.9), calls=%async_computation | async-start | bytes 2097152 | tf_op jit(solution)/shard_map/all_to_all | solution.py:163
  9.7 13.0 %collective-permute-start.1 = (f32[64,4096]{1,0:T(8,128)S(1)}, f32[64,4096]{1,0:T(8,128)}, u32[]{:S(2)}, u32[]{:S(2)}) collective-permute-start(f32[64,4096]{1,0:T(8,128)S(1)} %bitcast.12), channel_id=1, source_target_pairs={{0,1},{1,0},{2,3},{3,2},{4,5},{5,4},{6,7},{7,6},{8,9},{9,8},{10,11... | collective-permute-start | bytes 3145736 | tf_op jit(solution)/shard_map/ppermute | solution.py:178
  18.8 8.4 %collective-permute-start = (s32[2,1024]{1,0:T(2,128)S(1)}, s32[2,1024]{1,0:T(2,128)S(1)}, u32[]{:S(2)}, u32[]{:S(2)}) collective-permute-start(s32[2,1024]{1,0:T(2,128)S(1)} %pad_add_fusion.own_tasks_ref), channel_id=1, source_target_pairs={{0,1},{1,0},{2,3},{3,2},{4,5},{5,4},{6,7},{7,6},{8,9},{9,8},{10,11... | collective-permute-start | bytes 24584 | tf_op jit(solution)/shard_map/ppermute | solution.py:179
  25.9 1.3 %copy-start = (bf16[64,128,128]{2,1,0:T(8,128)(2,1)}, bf16[64,128,128]{2,1,0:T(8,128)(2,1)S(1)}, u32[]{:S(2)}) copy-start(bf16[64,128,128]{2,1,0:T(8,128)(2,1)S(1)} %split_rights.3.twin_ref) | copy-start | bytes 6291460
  34.0 1.6 %copy-start.1 = (bf16[64,128,128]{2,1,0:T(8,128)(2,1)S(1)}, bf16[64,128,128]{2,1,0:T(8,128)(2,1)}, u32[]{:S(2)}) copy-start(bf16[64,128,128]{2,1,0:T(8,128)(2,1)} %copy-done) | copy-start | bytes 6291460
  49.0 9.4 %collective-permute-start.2 = (f32[8,96,256]{2,1,0:T(8,128)S(1)}, f32[8,96,256]{2,1,0:T(8,128)S(1)}, u32[]{:S(2)}, u32[]{:S(2)}) collective-permute-start(f32[8,96,256]{2,1,0:T(8,128)S(1)} %get-tuple-element.8), channel_id=1, source_target_pairs={{0,1},{1,0},{2,3},{3,2},{4,5},{5,4},{6,7},{7,6},{8,9},{9,8},{10,11... | collective-permute-start | bytes 2359304 | tf_op jit(solution)/shard_map/ppermute | solution.py:183
  58.5 56.2 %copy-start.5 = (s32[1,96]{1,0:T(1,128)S(1)}, s32[1,96]{1,0:T(1,128)}, u32[]{:S(2)}) copy-start(s32[1,96]{1,0:T(1,128)} %param.9) | copy-start | bytes 1156
  85.3 29.4 %all-to-all-start.2 = ((f32[48,2,256]{2,1,0:T(2,128)}), f32[48,2,256]{2,1,0:T(2,128)S(1)}, u32[]{:S(2)}, u32[]{:S(2)}) async-start(f32[48,2,256]{2,1,0:T(2,128)} %reshape.35), calls=%async_computation.2 | async-start | bytes 196608 | tf_op jit(solution)/shard_map/all_to_all | solution.py:163

commit v3 on v2

v3 whole, which is shorter than its diff:
```python
import jax
import jax.numpy as jnp
from jax import lax
from jax.experimental import pallas as pl
from jax.experimental.pallas import tpu as pltpu
from jax.sharding import Mesh
from jax.sharding import PartitionSpec as P

BS = 64
BLK = BS * BS
OWN_DEV = 2
CAPACITY = 2
COLUMNS = 4
VMEM_LIMIT = 24 * 1024 * 1024
ROWS = BLK // 128
FLAT = ROWS + 8
SWAP = [(0, 1), (1, 0)]


def low_half(shape):
    return lax.broadcasted_iota(jnp.int32, shape, len(shape) - 1) < BS


def split_rights(own_ref, twin_ref, parts_ref, spread_ref):
    count = own_ref.shape[0]
    mask = low_half((8, 128))

    for side, right_ref in enumerate((own_ref, twin_ref)):

        def unfold(group, carry, right_ref=right_ref, side=side):
            base = pl.multiple_of(group * 8, 8)
            spot = (side * count + base) * BS
            for m in range(ROWS):
                x = right_ref[pl.ds(base, 8), m * 128 : (m + 1) * 128]
                turned = pltpu.roll(x, BS, 1)
                spread_ref[pl.ds(spot + 2 * m, 8, stride=BS), :] = jnp.where(mask, x, turned)
                spread_ref[pl.ds(spot + 2 * m + 1, 8, stride=BS), :] = jnp.where(mask, turned, x)
            return carry

        lax.fori_loop(0, count // 8, unfold, 0)

    def cut(block, carry):
        x = spread_ref[pl.ds(pl.multiple_of(block * BS, BS), BS), :]
        coarse = x.astype(jnp.bfloat16)
        parts_ref[block, :BS, :] = coarse
        parts_ref[block, BS:, :] = (x - coarse.astype(jnp.float32)).astype(jnp.bfloat16)
        return carry

    lax.fori_loop(0, 2 * count, cut, 0, unroll=4)


def prepare(own, twin):
    count = own.shape[0]
    return pl.pallas_call(
        split_rights,
        out_shape=jax.ShapeDtypeStruct((2 * count, 2 * BS, 128), jnp.bfloat16),
        in_specs=[pl.BlockSpec(memory_space=pltpu.VMEM)] * 2,
        out_specs=pl.BlockSpec(memory_space=pltpu.VMEM),
        scratch_shapes=[pltpu.VMEM((2 * count * BS, 128), jnp.float32)],
        compiler_params=pltpu.CompilerParams(vmem_limit_bytes=VMEM_LIMIT),
        cost_estimate=pl.CostEstimate(flops=16 * count * BLK, bytes_accessed=24 * count * BLK, transcendentals=0),
        name="split_rights",
    )(own, twin)


def copy_out(x_ref, out_hbm, sems):
    copies = [pltpu.make_async_copy(x_ref, out_hbm.at[i], sems.at[i]) for i in range(out_hbm.shape[0])]
    for copy in copies:
        copy.start()
    for copy in copies:
        copy.wait()


def repeat(x, count):
    return pl.pallas_call(
        copy_out,
        out_shape=jax.ShapeDtypeStruct((count,) + x.shape, x.dtype),
        in_specs=[pl.BlockSpec(memory_space=pltpu.VMEM)],
        out_specs=pl.BlockSpec(memory_space=pltpu.HBM),
        scratch_shapes=[pltpu.SemaphoreType.DMA((count,))],
        name="repeat",
    )(x)


def multiply(
    core_ref, own_tasks_hbm, twin_tasks_hbm, left_ref, parts_hbm, mine_ref, other_ref,
    own_tasks_ref, twin_tasks_ref, parts_ref, flat_ref, lhs_ref, acc0, acc1, nat_ref, sems,
):
    copies = [
        pltpu.make_async_copy(source, target, sems.at[i])
        for i, (source, target) in enumerate(
            ((own_tasks_hbm, own_tasks_ref), (twin_tasks_hbm, twin_tasks_ref), (parts_hbm, parts_ref))
        )
    ]
    for copy in copies:
        copy.start()
    chips, share = left_ref.shape[0], left_ref.shape[1]
    count = chips * share
    per_block = own_tasks_ref.shape[1] // (2 * count)
    slot_count = acc0.shape[0]
    rights = parts_ref.shape[0] // 2
    core = core_ref[0]

    def clear(s, carry):
        acc0[s] = jnp.zeros(acc0.shape[1:], jnp.float32)
        acc1[s] = jnp.zeros(acc1.shape[1:], jnp.float32)
        return carry

    lax.fori_loop(0, slot_count, clear, 0, unroll=8)

    def unfold(chip, carry):
        for m in range(ROWS):
            flat_ref[pl.ds(chip * share * FLAT + m, share, stride=FLAT), :] = left_ref[chip, :, m * 128 : (m + 1) * 128]
        return carry

    lax.fori_loop(0, chips, unfold, 0)
    mask = low_half((ROWS, 128))
    wide = low_half((2 * BS, 128))

    def cut(k, carry):
        x = flat_ref[pl.ds(pl.multiple_of(k * FLAT, 8), ROWS), :]
        coarse = x.astype(jnp.bfloat16).astype(jnp.float32)
        fine = x - coarse
        lhs_ref[k, :ROWS, :] = jnp.where(mask, coarse, pltpu.roll(fine, BS, 1)).astype(jnp.bfloat16)
        lhs_ref[k, ROWS:, :] = jnp.where(mask, pltpu.roll(coarse, BS, 1), fine).astype(jnp.bfloat16)
        return carry

    lax.fori_loop(0, count, cut, 0, unroll=8)
    for copy in copies:
        copy.wait()

    def one_block(k, carry):
        tall = lhs_ref[k]
        lhs = jnp.concatenate([tall, tall], axis=1)
        first = ((k // share) * 2 * share + core * share + k % share) * per_block
        for side, tasks_ref in enumerate((own_tasks_ref, twin_tasks_ref)):
            for quad in range(per_block // 4):
                pairs = []
                for pair in range(2):
                    t = first + quad * 4 + pair * 2
                    low = parts_ref[side * rights + tasks_ref[0, t]]
                    high = parts_ref[side * rights + tasks_ref[0, t + 1]]
                    pairs.append(jnp.where(wide, low, high))
                both = jnp.concatenate(pairs, axis=1)
                rhs = jnp.concatenate([both[:BS], both[:BS], both[BS:], both[BS:]], axis=0)
                out = jnp.dot(lhs, rhs, preferred_element_type=jnp.float32)
                for pair in range(2):
                    t = first + quad * 4 + pair * 2
                    part = out[:, pair * 128 : (pair + 1) * 128]
                    acc0[tasks_ref[1, t]] += part
                    acc1[tasks_ref[1, t + 1]] += part
        return carry

    lax.fori_loop(0, count, one_block, 0, unroll=16)

    columns, _, run = mine_ref.shape[:3]
    capacity = CAPACITY

    def fold(s, carry):
        owner = s // capacity
        spot = (owner % columns) * run + (owner // columns) * capacity + s % capacity
        low, high = acc0[s], acc1[s]
        even = low[:ROWS] + pltpu.roll(high[:ROWS], BS, 1)
        odd = pltpu.roll(low[ROWS:], BS, 1) + high[ROWS:]
        nat_ref[pl.ds(pl.multiple_of(spot * FLAT, 8), ROWS), :] = jnp.where(mask, even, odd)
        return carry

    lax.fori_loop(0, slot_count, fold, 0, unroll=16)

    tiles = ROWS // (2 * chips)

    def place(column, carry):
        for group in range(run // 8):
            for out_ref, half in ((mine_ref, core), (other_ref, 1 - core)):
                first = (column * run + group * 8) * FLAT + half * (ROWS // 2)
                for m in range(ROWS // 2):
                    out_ref[column, m // tiles, group * 8 : (group + 1) * 8, (m % tiles) * 128 : (m % tiles + 1) * 128] = (
                        nat_ref[pl.ds(first + m, 8, stride=FLAT), :]
                    )
        return carry

    lax.fori_loop(0, columns, place, 0)


def products(core, own_tasks, twin_tasks, panel, parts, slot_count, columns):
    chips, share, _ = panel.shape
    smem = pl.BlockSpec(memory_space=pltpu.SMEM)
    vmem = pl.BlockSpec(memory_space=pltpu.VMEM)
    anywhere = pl.BlockSpec(memory_space=pl.ANY)
    acc = pltpu.VMEM((slot_count, BS, 128), jnp.float32)
    out = jax.ShapeDtypeStruct((columns, chips, slot_count // columns, BLK // (2 * chips)), jnp.float32)
    flops = 2 * own_tasks.shape[1] * BS * BS * BS * 4
    return pl.pallas_call(
        multiply,
        out_shape=(out, out),
        in_specs=[smem, anywhere, anywhere, vmem, pl.BlockSpec(memory_space=pltpu.HBM)],
        out_specs=(vmem, vmem),
        scratch_shapes=[
            pltpu.SMEM(own_tasks.shape, jnp.int32),
            pltpu.SMEM(twin_tasks.shape, jnp.int32),
            pltpu.VMEM(parts.shape, parts.dtype),
            pltpu.VMEM((chips * share * FLAT, 128), jnp.float32),
            pltpu.VMEM((chips * share, BS, 128), jnp.bfloat16),
            acc,
            acc,
            pltpu.VMEM((slot_count * FLAT, 128), jnp.float32),
            pltpu.SemaphoreType.DMA((3,)),
        ],
        compiler_params=pltpu.CompilerParams(vmem_limit_bytes=VMEM_LIMIT),
        cost_estimate=pl.CostEstimate(flops=flops, bytes_accessed=8 * 1024 * 1024, transcendentals=0),
        name="multiply",
    )(core, own_tasks, twin_tasks, panel, parts)


def exchange(x, axis):
    return lax.all_to_all(x, axis, split_axis=0, concat_axis=0, tiled=True)


def local(left_blocks, right_blocks, task_right, task_slot, recv_owner):
    columns, chips = lax.axis_size("x"), lax.axis_size("y")
    layers = lax.axis_size("z")
    group = ("y", "core")
    members = 2 * chips
    slot_count = recv_owner.shape[1]
    core = lax.axis_index("core").astype(jnp.int32).reshape(1)

    panel = exchange(repeat(left_blocks[0], chips), "y")
    rights = right_blocks[0, 0]
    tasks = jnp.concatenate([task_right[0], task_slot[0]], axis=0)
    twin_tasks = lax.ppermute(tasks, "core", SWAP)
    parts = pltpu.with_memory_space_constraint(prepare(rights, lax.ppermute(rights, "core", SWAP)), pltpu.HBM)
    mine, other = products(core, tasks, twin_tasks, panel, parts, slot_count, columns)
    mine = mine + lax.ppermute(other, "core", SWAP)
    run, width = mine.shape[2:]
    pieces = exchange(mine.reshape(columns * chips, run, width), ("x", "y"))
    piece = pieces.reshape(columns, chips, run, width).sum(axis=1).reshape(columns, layers, CAPACITY, width)
    piece = piece.transpose(1, 0, 2, 3).reshape(layers, columns * CAPACITY, width)
    received = exchange(piece, "z").reshape(slot_count, width)
    owners = recv_owner[0]
    owned_ids = jnp.arange(OWN_DEV * members, dtype=jnp.int32)
    selector = (owners[None, :] == owned_ids[:, None]).astype(jnp.float32)
    owned = jnp.dot(selector, received, precision=lax.Precision.HIGHEST, preferred_element_type=jnp.float32)
    own_blocks = exchange(owned.reshape(members, OWN_DEV, width), group)
    own_blocks = own_blocks.reshape(chips, 2, OWN_DEV, width).transpose(2, 1, 0, 3)
    return own_blocks.reshape(1, OWN_DEV, BLK)


def solution(mesh):
    rows, reps = mesh.shape["row"], mesh.shape["rep"]
    fine = Mesh(mesh.devices.reshape(rows // COLUMNS, COLUMNS, reps // 2, 2), ("z", "x", "y", "core"))
    row = ("z", "x")
    group = ("y", "core")
    in_specs = (
        P(row, group, None),
        P(row, group, None, None),
        P(row, group, None),
        P(row, group, None),
        P(row, None),
    )
    out_specs = P(row, group, None)
    return jax.shard_map(local, mesh=fine, in_specs=in_specs, out_specs=out_specs, check_vma=False)
```

time: 128 us -> 122 us (0.953)
  starting transfers between devices: 44.1 us -> 39.5 us
  Pallas kernels: 18.6 us -> 16.2 us
  blocking collectives: 38.3 us -> 40.6 us
  local copies, waits for them, and re-layouts: 6.43 us -> 4.62 us
    all_to_all x2, starting transfers between devices: 25.6 us -> 22.5 us  [exchange(): return lax.all_to_all(x, axis, split_axis=0, concat_axis=0, tiled=True)]
    pallas_call x3, Pallas kernels: 18.6 us -> 16.2 us  [the longest x1 10.4 us: products(): pl.pallas_call(multiply, out_shape=(out, out), in_specs=[smem, anywhere,...]
    all_to_all x2, blocking collectives: 38.3 us -> 40.6 us  [exchange(): return lax.all_to_all(x, axis, split_axis=0, concat_axis=0, tiled=True)]
    broadcast_in_dim x1 -> x0, local copies, waits for them, and re-layouts: 2.06 us -> none  [local(): jnp.broadcast_to(left_blocks, (chips,) + left_blocks.shape[1:])]
    unnamed x12 -> x6, local copies, waits for them, and re-layouts: 2.93 us -> 3.15 us
  transfers between devices with their start and end apart: 5 -> 5, of which waited for: 3 -> 3; matrix products, arithmetic and copies ran while one was open for 0% -> 1% of each run, Pallas kernels for 4% -> 3%
where the time goes in v3:
time: 122 us; the launch traced here: 121 us
  blocking collectives  40.6 us (33%)
  starting transfers between devices  39.5 us (32%)
  waiting for transfers between devices  18.8 us (15%)
  Pallas kernels  16.2 us (13%)
  local copies, waits for them, and re-layouts  4.62 us (4%)
    all_to_all x2, blocking collectives, exchange(): return lax.all_to_all(x, axis, split_axis=0, concat_axis=0, tiled=True)  40.6 us
    all_to_all x2, starting transfers between devices, exchange(): return lax.all_to_all(x, axis, split_axis=0, concat_axis=0, tiled=True)  22.5 us
    all_to_all x2, waiting for transfers between devices, exchange(): return lax.all_to_all(x, axis, split_axis=0, concat_axis=0, tiled=True)  16.9 us
    pallas_call x1, Pallas kernels, products(): pl.pallas_call(multiply, out_shape=(out, out), in_specs=[smem, anywhere,...  10.4 us
    ppermute x1, starting transfers between devices, local(): lax.ppermute(rights, 'core', SWAP)  8.34 us
    ppermute x1, starting transfers between devices, local(): mine = mine + lax.ppermute(other, 'core', SWAP)  6.74 us
    pallas_call x1, Pallas kernels, prepare(): pl.pallas_call(split_rights, out_shape=jax.ShapeDtypeStruct((2 * count, 2...  3.92 us
    unnamed x6, local copies, waits for them, and re-layouts  3.15 us
  transfers between devices with their start and end apart: 5, of which 3 were waited for; matrix products, arithmetic and copies ran while one was open for 1% of the time, Pallas kernels for 3%

profile of v3, /device:TPU:1, one launch (start us, length us, event | category | flops | bytes accessed | tf_op | source)
XLA Modules:
  0.0 121.1 jit_solution(15321712865385836793)
XLA Ops:
  0.0 1.9 %repeat.1 = f32[8,8,4096]{2,1,0:T(8,128)} custom-call(f32[8,4096]{1,0:T(8,128)} %bitcast.26), custom_call_target="tpu_custom_call" | custom-call | tf_op jit(solution)/shard_map/repeat/pallas_call | solution.py:75
  1.9 7.7 %all-to-all-start = ((f32[8,8,4096]{2,1,0:T(8,128)}), f32[8,8,4096]{2,1,0:T(8,128)S(1)}, u32[]{:S(2)}, u32[]{:S(2)}) async-start(f32[8,8,4096]{2,1,0:T(8,128)} %repeat.1), calls=%async_computation | async-start | bytes 2097152 | tf_op jit(solution)/shard_map/all_to_all | solution.py:216
  9.6 8.3 %collective-permute-start.1 = (f32[64,4096]{1,0:T(8,128)}, f32[64,4096]{1,0:T(8,128)S(1)}, u32[]{:S(2)}, u32[]{:S(2)}) collective-permute-start(f32[64,4096]{1,0:T(8,128)} %bitcast.22), channel_id=1, source_target_pairs={{0,1},{1,0},{2,3},{3,2},{4,5},{5,4},{6,7},{7,6},{8,9},{9,8},{10,11... | collective-permute-start | bytes 3145736 | tf_op jit(solution)/shard_map/ppermute | solution.py:231
  18.0 0.7 pad_add_fusion.own_tasks_hbm
  18.7 1.9 %collective-permute-start = (s32[2,1024]{1,0:T(2,128)S(1)}, s32[2,1024]{1,0:T(2,128)S(1)}, u32[]{:S(2)}, u32[]{:S(2)}) collective-permute-start(s32[2,1024]{1,0:T(2,128)S(1)} %pad_add_fusion.own_tasks_hbm), channel_id=1, source_target_pairs={{0,1},{1,0},{2,3},{3,2},{4,5},{5,4},{6,7},{7,6},{8,9},{9,8},{10,11... | collective-permute-start | bytes 24584 | tf_op jit(solution)/shard_map/ppermute | solution.py:230
  20.6 0.0 collective-permute-done.1.twin_ref
  20.6 0.0 copy-start.1
  20.6 1.2 %copy-done.1 = f32[1,1,64,4096]{3,2,1,0:T(8,128)S(1)} copy-done((f32[1,1,64,4096]{3,2,1,0:T(8,128)S(1)}, f32[1,1,64,4096]{3,2,1,0:T(8,128)}, u32[]{:S(2)}) %copy-start.1) | copy-done | bytes 1048600
  21.8 3.9 %split_rights.1.parts_hbm = bf16[128,128,128]{2,1,0:T(8,128)(2,1)S(1)} custom-call(f32[64,4096]{1,0:T(8,128)S(1)} %bitcast.23, f32[64,4096]{1,0:T(8,128)S(1)} %collective-permute-done.1.twin_ref), custom_call_target="tpu_custom_call" | custom-call | flops 4194304 | bytes 6291456 | tf_op jit(solution)/shard_map/split_rights/pallas_call | solution.py:54
  25.8 0.0 copy-start
  25.8 1.9 %copy-done = bf16[128,128,128]{2,1,0:T(8,128)(2,1)} copy-done((bf16[128,128,128]{2,1,0:T(8,128)(2,1)}, bf16[128,128,128]{2,1,0:T(8,128)(2,1)S(1)}, u32[]{:S(2)}) %copy-start) | copy-done | bytes 4194328
  27.7 0.0 collective-permute-done.twin_tasks_hbm
  27.7 6.8 %all-to-all-done.left_ref = f32[8,8,4096]{2,1,0:T(8,128)S(1)} async-done(((f32[8,8,4096]{2,1,0:T(8,128)}), f32[8,8,4096]{2,1,0:T(8,128)S(1)}, u32[]{:S(2)}, u32[]{:S(2)}) %all-to-all-start) | async-done | bytes 1048608 | tf_op jit(solution)/shard_map/all_to_all | solution.py:216
  34.5 10.4 %multiply.5 = (f32[4,8,24,256]{3,2,1,0:T(8,128)S(1)}, f32[4,8,24,256]{3,2,1,0:T(8,128)S(1)}) custom-call(s32[1]{0:T(128)} %bitcast.1.core_ref, s32[2,1024]{1,0:T(2,128)S(1)} %pad_add_fusion.own_tasks_hbm, s32[2,1024]{1,0:T(2,128)S(1)} %collective-permute-done.twin_tasks_hbm, f32[8,8,4096]{2,1,0:T(8,128)S(1)} %all-to-all-done.left_ref, ...), custom_call_target="tpu_custom_call" | custom-call | flops 2147483648 | bytes 8388608 | tf_op jit(solution)/shard_map/multiply/pallas_call | solution.py:193
  44.9 0.0 copy-start.2
  44.9 6.7 %collective-permute-start.2 = (f32[4,8,24,256]{3,2,1,0:T(8,128)S(1)}, f32[4,8,24,256]{3,2,1,0:T(8,128)S(1)}, u32[]{:S(2)}, u32[]{:S(2)}) collective-permute-start(f32[4,8,24,256]{3,2,1,0:T(8,128)S(1)} %get-tuple-element.8), channel_id=1, source_target_pairs={{0,1},{1,0},{2,3},{3,2},{4,5},{5,4},{6,7},{7,6},{8,9},{9,8},{10,11... | collective-permute-start | bytes 2359304 | tf_op jit(solution)/shard_map/ppermute | solution.py:233
  51.7 1.9 %collective-permute-done.2 = f32[4,8,24,256]{3,2,1,0:T(8,128)S(1)} collective-permute-done((f32[4,8,24,256]{3,2,1,0:T(8,128)S(1)}, f32[4,8,24,256]{3,2,1,0:T(8,128)S(1)}, u32[]{:S(2)}, u32[]{:S(2)}) %collective-permute-start.2) | collective-permute-done | bytes 786464 | tf_op jit(solution)/shard_map/ppermute | solution.py:233
  53.6 0.1 add.7
  53.7 23.0 %all_to_all.20 = f32[32,24,256]{2,1,0:T(8,128)S(1)} all-to-all(f32[32,24,256]{2,1,0:T(8,128)S(1)} %bitcast.24), channel_id=1, replica_groups=mesh['z'=12,'x'=4,'y'=8,'core'=2] {'x','y'}, dimensions={0} | all-to-all | bytes 1572864 | tf_op jit(solution)/shard_map/all_to_all | solution.py:216
  76.8 0.1 copy.11
  76.9 0.7 reshape.47
  77.6 14.9 %all-to-all-start.2 = ((f32[12,8,256]{2,1,0:T(8,128)}), f32[12,8,256]{2,1,0:T(8,128)S(1)}, u32[]{:S(2)}, u32[]{:S(2)}) async-start(f32[12,8,256]{2,1,0:T(8,128)} %reshape.47), calls=%async_computation.2 | async-start | bytes 196608 | tf_op jit(solution)/shard_map/all_to_all | solution.py:216
  92.5 10.1 %all-to-all-done.2 = f32[12,8,256]{2,1,0:T(8,128)S(1)} async-done(((f32[12,8,256]{2,1,0:T(8,128)}), f32[12,8,256]{2,1,0:T(8,128)S(1)}, u32[]{:S(2)}, u32[]{:S(2)}) %all-to-all-start.2) | async-done | bytes 98336 | tf_op jit(solution)/shard_map/all_to_all | solution.py:216
  102.6 0.0 copy-done.2
  102.6 0.2 fusion
  102.8 17.6 %all_to_all.21 = f32[16,2,256]{2,1,0:T(2,128)S(1)} all-to-all(f32[16,2,256]{2,1,0:T(2,128)S(1)} %copy.12), channel_id=1, replica_groups=mesh['z'=12,'x'=4,'y'=8,'core'=2] {'y','core'}, dimensions={0} | all-to-all | bytes 65536 | tf_op jit(solution)/shard_map/all_to_all | solution.py:216
  120.4 0.6 reshape.50
  (5 shorter events, 0.1 us)
Async XLA Ops:
  1.9 32.6 %all-to-all-start = ((f32[8,8,4096]{2,1,0:T(8,128)}), f32[8,8,4096]{2,1,0:T(8,128)S(1)}, u32[]{:S(2)}, u32[]{:S(2)}) async-start(f32[8,8,4096]{2,1,0:T(8,128)} %repeat.1), calls=%async_computation | async-start | bytes 2097152 | tf_op jit(solution)/shard_map/all_to_all | solution.py:216
  9.6 11.0 %collective-permute-start.1 = (f32[64,4096]{1,0:T(8,128)}, f32[64,4096]{1,0:T(8,128)S(1)}, u32[]{:S(2)}, u32[]{:S(2)}) collective-permute-start(f32[64,4096]{1,0:T(8,128)} %bitcast.22), channel_id=1, source_target_pairs={{0,1},{1,0},{2,3},{3,2},{4,5},{5,4},{6,7},{7,6},{8,9},{9,8},{10,11... | collective-permute-start | bytes 3145736 | tf_op jit(solution)/shard_map/ppermute | solution.py:231
  18.7 9.0 %collective-permute-start = (s32[2,1024]{1,0:T(2,128)S(1)}, s32[2,1024]{1,0:T(2,128)S(1)}, u32[]{:S(2)}, u32[]{:S(2)}) collective-permute-start(s32[2,1024]{1,0:T(2,128)S(1)} %pad_add_fusion.own_tasks_hbm), channel_id=1, source_target_pairs={{0,1},{1,0},{2,3},{3,2},{4,5},{5,4},{6,7},{7,6},{8,9},{9,8},{10,11... | collective-permute-start | bytes 24584 | tf_op jit(solution)/shard_map/ppermute | solution.py:230
  20.6 1.2 %copy-start.1 = (f32[1,1,64,4096]{3,2,1,0:T(8,128)S(1)}, f32[1,1,64,4096]{3,2,1,0:T(8,128)}, u32[]{:S(2)}) copy-start(f32[1,1,64,4096]{3,2,1,0:T(8,128)} %param.6) | copy-start | bytes 3145732
  25.8 1.9 %copy-start = (bf16[128,128,128]{2,1,0:T(8,128)(2,1)}, bf16[128,128,128]{2,1,0:T(8,128)(2,1)S(1)}, u32[]{:S(2)}) copy-start(bf16[128,128,128]{2,1,0:T(8,128)(2,1)S(1)} %split_rights.1.parts_hbm) | copy-start | bytes 12582916
  44.9 57.7 %copy-start.2 = (s32[1,96]{1,0:T(1,128)S(1)}, s32[1,96]{1,0:T(1,128)}, u32[]{:S(2)}) copy-start(s32[1,96]{1,0:T(1,128)} %param.9) | copy-start | bytes 1156
  44.9 8.6 %collective-permute-start.2 = (f32[4,8,24,256]{3,2,1,0:T(8,128)S(1)}, f32[4,8,24,256]{3,2,1,0:T(8,128)S(1)}, u32[]{:S(2)}, u32[]{:S(2)}) collective-permute-start(f32[4,8,24,256]{3,2,1,0:T(8,128)S(1)} %get-tuple-element.8), channel_id=1, source_target_pairs={{0,1},{1,0},{2,3},{3,2},{4,5},{5,4},{6,7},{7,6},{8,9},{9,8},{10,11... | collective-permute-start | bytes 2359304 | tf_op jit(solution)/shard_map/ppermute | solution.py:233
  77.6 25.0 %all-to-all-start.2 = ((f32[12,8,256]{2,1,0:T(8,128)}), f32[12,8,256]{2,1,0:T(8,128)S(1)}, u32[]{:S(2)}, u32[]{:S(2)}) async-start(f32[12,8,256]{2,1,0:T(8,128)} %reshape.47), calls=%async_computation.2 | async-start | bytes 196608 | tf_op jit(solution)/shard_map/all_to_all | solution.py:216

commit v4 on v3

--- a/solution.py
+++ b/solution.py
@@ -153,7 +153,7 @@
 
     lax.fori_loop(0, count, one_block, 0, unroll=16)
 
-    columns, _, run = mine_ref.shape[:3]
+    _, columns, run = mine_ref.shape[:3]
     capacity = CAPACITY
 
     def fold(s, carry):
@@ -174,7 +174,7 @@
             for out_ref, half in ((mine_ref, core), (other_ref, 1 - core)):
                 first = (column * run + group * 8) * FLAT + half * (ROWS // 2)
                 for m in range(ROWS // 2):
-                    out_ref[column, m // tiles, group * 8 : (group + 1) * 8, (m % tiles) * 128 : (m % tiles + 1) * 128] = (
+                    out_ref[m // tiles, column, group * 8 : (group + 1) * 8, (m % tiles) * 128 : (m % tiles + 1) * 128] = (
                         nat_ref[pl.ds(first + m, 8, stride=FLAT), :]
                     )
         return carry
@@ -188,7 +188,7 @@
     vmem = pl.BlockSpec(memory_space=pltpu.VMEM)
     anywhere = pl.BlockSpec(memory_space=pl.ANY)
     acc = pltpu.VMEM((slot_count, BS, 128), jnp.float32)
-    out = jax.ShapeDtypeStruct((columns, chips, slot_count // columns, BLK // (2 * chips)), jnp.float32)
+    out = jax.ShapeDtypeStruct((chips, columns, slot_count // columns, BLK // (2 * chips)), jnp.float32)
     flops = 2 * own_tasks.shape[1] * BS * BS * BS * 4
     return pl.pallas_call(
         multiply,
@@ -228,21 +228,21 @@
     rights = right_blocks[0, 0]
     tasks = jnp.concatenate([task_right[0], task_slot[0]], axis=0)
     twin_tasks = lax.ppermute(tasks, "core", SWAP)
-    parts = pltpu.with_memory_space_constraint(prepare(rights, lax.ppermute(rights, "core", SWAP)), pltpu.HBM)
+    owned_ids = jnp.arange(OWN_DEV * members, dtype=jnp.int32).reshape(chips, 2, OWN_DEV).transpose(1, 0, 2).reshape(-1)
+    selector = (recv_owner[0][None, :] == owned_ids[:, None]).astype(jnp.float32)
+    parts = prepare(rights, lax.ppermute(rights, "core", SWAP))
+    parts, selector = lax.optimization_barrier((parts, selector))
+    parts = pltpu.with_memory_space_constraint(parts, pltpu.HBM)
     mine, other = products(core, tasks, twin_tasks, panel, parts, slot_count, columns)
     mine = mine + lax.ppermute(other, "core", SWAP)
     run, width = mine.shape[2:]
-    pieces = exchange(mine.reshape(columns * chips, run, width), ("x", "y"))
-    piece = pieces.reshape(columns, chips, run, width).sum(axis=1).reshape(columns, layers, CAPACITY, width)
+    pieces = exchange(mine.reshape(chips * columns, run, width), ("y", "x"))
+    piece = pieces.reshape(chips, columns, run, width).sum(axis=0).reshape(columns, layers, CAPACITY, width)
     piece = piece.transpose(1, 0, 2, 3).reshape(layers, columns * CAPACITY, width)
     received = exchange(piece, "z").reshape(slot_count, width)
-    owners = recv_owner[0]
-    owned_ids = jnp.arange(OWN_DEV * members, dtype=jnp.int32)
-    selector = (owners[None, :] == owned_ids[:, None]).astype(jnp.float32)
     owned = jnp.dot(selector, received, precision=lax.Precision.HIGHEST, preferred_element_type=jnp.float32)
-    own_blocks = exchange(owned.reshape(members, OWN_DEV, width), group)
-    own_blocks = own_blocks.reshape(chips, 2, OWN_DEV, width).transpose(2, 1, 0, 3)
-    return own_blocks.reshape(1, OWN_DEV, BLK)
+    own_blocks = exchange(owned.reshape(members, OWN_DEV, width), ("core", "y"))
+    return own_blocks.transpose(1, 0, 2).reshape(1, OWN_DEV, BLK)
 
 
 def solution(mesh):

time: 122 us -> 120 us (0.984)
  blocking collectives: 40.6 us -> 64.6 us
  starting transfers between devices: 39.5 us -> 24.7 us
  waiting for transfers between devices: 18.8 us -> 7.87 us
    all_to_all x2 -> x3, blocking collectives: 40.6 us -> 64.6 us  [exchange(): return lax.all_to_all(x, axis, split_axis=0, concat_axis=0, tiled=True)]
    all_to_all x2 -> x1, starting transfers between devices: 22.5 us -> 7.66 us  [exchange(): return lax.all_to_all(x, axis, split_axis=0, concat_axis=0, tiled=True)]
    all_to_all x2 -> x1, waiting for transfers between devices: 16.9 us -> 5.98 us  [exchange(): return lax.all_to_all(x, axis, split_axis=0, concat_axis=0, tiled=True)]
    unnamed x6 -> x5, local copies, waits for them, and re-layouts: 3.15 us -> 3.76 us
  transfers between devices with their start and end apart: 5 -> 4, of which waited for: 3 -> 2; matrix products, arithmetic and copies ran while one was open for 1% -> 1% of each run, Pallas kernels for 3% -> 3%
where the time goes in v4:
time: 120 us; the launch traced here: 119 us
  blocking collectives  64.6 us (54%)
  starting transfers between devices  24.7 us (21%)
  Pallas kernels  16.3 us (14%)
  waiting for transfers between devices  7.87 us (7%)
  local copies, waits for them, and re-layouts  4.04 us (3%)
  other arithmetic  1.61 us (1%)
    all_to_all x3, blocking collectives, exchange(): return lax.all_to_all(x, axis, split_axis=0, concat_axis=0, tiled=True)  64.6 us
    pallas_call x1, Pallas kernels, products(): pl.pallas_call(multiply, out_shape=(out, out), in_specs=[smem, anywhere,...  10.4 us
    ppermute x1, starting transfers between devices, local(): parts = prepare(rights, lax.ppermute(rights, 'core', SWAP))  8.34 us
    all_to_all x1, starting transfers between devices, exchange(): return lax.all_to_all(x, axis, split_axis=0, concat_axis=0, tiled=True)  7.66 us
    ppermute x1, starting transfers between devices, local(): mine = mine + lax.ppermute(other, 'core', SWAP)  6.74 us
    all_to_all x1, waiting for transfers between devices, exchange(): return lax.all_to_all(x, axis, split_axis=0, concat_axis=0, tiled=True)  5.98 us
    pallas_call x1, Pallas kernels, prepare(): pl.pallas_call(split_rights, out_shape=jax.ShapeDtypeStruct((2 * count, 2...  3.92 us
    unnamed x5, local copies, waits for them, and re-layouts  3.76 us
  transfers between devices with their start and end apart: 4, of which 2 were waited for; matrix products, arithmetic and copies ran while one was open for 1% of the time, Pallas kernels for 3%

profile of v4, /device:TPU:1, one launch (start us, length us, event | category | flops | bytes accessed | tf_op | source)
XLA Modules:
  0.0 119.4 jit_solution(17367872127541870646)
XLA Ops:
  0.0 2.0 %repeat.1 = f32[8,8,4096]{2,1,0:T(8,128)} custom-call(f32[8,4096]{1,0:T(8,128)} %bitcast.25), custom_call_target="tpu_custom_call" | custom-call | tf_op jit(solution)/shard_map/repeat/pallas_call | solution.py:75
  2.0 7.7 %all-to-all-start = ((f32[8,8,4096]{2,1,0:T(8,128)}), f32[8,8,4096]{2,1,0:T(8,128)S(1)}, u32[]{:S(2)}, u32[]{:S(2)}) async-start(f32[8,8,4096]{2,1,0:T(8,128)} %repeat.1), calls=%async_computation | async-start | bytes 2097152 | tf_op jit(solution)/shard_map/all_to_all | solution.py:216
  9.6 8.3 %collective-permute-start = (f32[64,4096]{1,0:T(8,128)}, f32[64,4096]{1,0:T(8,128)S(1)}, u32[]{:S(2)}, u32[]{:S(2)}) collective-permute-start(f32[64,4096]{1,0:T(8,128)} %bitcast.20), channel_id=1, source_target_pairs={{0,1},{1,0},{2,3},{3,2},{4,5},{5,4},{6,7},{7,6},{8,9},{9,8},{10,11... | collective-permute-start | bytes 3145736 | tf_op jit(solution)/shard_map/ppermute | solution.py:233
  18.0 0.7 pad_add_fusion.own_tasks_hbm
  18.7 1.9 %collective-permute-start.1 = (s32[2,1024]{1,0:T(2,128)S(1)}, s32[2,1024]{1,0:T(2,128)S(1)}, u32[]{:S(2)}, u32[]{:S(2)}) collective-permute-start(s32[2,1024]{1,0:T(2,128)S(1)} %pad_add_fusion.own_tasks_hbm), channel_id=1, source_target_pairs={{0,1},{1,0},{2,3},{3,2},{4,5},{5,4},{6,7},{7,6},{8,9},{9,8},{10,11... | collective-permute-start | bytes 24584 | tf_op jit(solution)/shard_map/ppermute | solution.py:230
  20.6 0.1 reshape.72
  20.7 0.7 compare_convert_fusion
  21.4 0.0 collective-permute-done.twin_ref
  21.4 0.0 copy-start.1
  21.5 1.2 %copy-done.1 = f32[1,1,64,4096]{3,2,1,0:T(8,128)S(1)} copy-done((f32[1,1,64,4096]{3,2,1,0:T(8,128)S(1)}, f32[1,1,64,4096]{3,2,1,0:T(8,128)}, u32[]{:S(2)}) %copy-start.1) | copy-done | bytes 1048600
  22.7 3.9 %split_rights.1.parts_hbm = bf16[128,128,128]{2,1,0:T(8,128)(2,1)S(1)} custom-call(f32[64,4096]{1,0:T(8,128)S(1)} %bitcast.21, f32[64,4096]{1,0:T(8,128)S(1)} %collective-permute-done.twin_ref), custom_call_target="tpu_custom_call" | custom-call | flops 4194304 | bytes 6291456 | tf_op jit(solution)/shard_map/split_rights/pallas_call | solution.py:54
  26.6 0.0 copy-start
  26.6 1.9 %copy-done = bf16[128,128,128]{2,1,0:T(8,128)(2,1)} copy-done((bf16[128,128,128]{2,1,0:T(8,128)(2,1)}, bf16[128,128,128]{2,1,0:T(8,128)(2,1)S(1)}, u32[]{:S(2)}) %copy-start) | copy-done | bytes 4194328
  28.5 0.0 collective-permute-done.1.twin_tasks_hbm
  28.5 6.0 %all-to-all-done.left_ref = f32[8,8,4096]{2,1,0:T(8,128)S(1)} async-done(((f32[8,8,4096]{2,1,0:T(8,128)}), f32[8,8,4096]{2,1,0:T(8,128)S(1)}, u32[]{:S(2)}, u32[]{:S(2)}) %all-to-all-start) | async-done | bytes 1048608 | tf_op jit(solution)/shard_map/all_to_all | solution.py:216
  34.5 10.4 %multiply.15 = (f32[8,4,24,256]{3,2,1,0:T(8,128)S(1)}, f32[8,4,24,256]{3,2,1,0:T(8,128)S(1)}) custom-call(s32[1]{0:T(128)} %bitcast.3.core_ref, s32[2,1024]{1,0:T(2,128)S(1)} %pad_add_fusion.own_tasks_hbm, s32[2,1024]{1,0:T(2,128)S(1)} %collective-permute-done.1.twin_tasks_hbm, f32[8,8,4096]{2,1,0:T(8,128)S(1)} %all-to-all-done.left_ref, ...), custom_call_target="tpu_custom_call" | custom-call | flops 2147483648 | bytes 8388608 | tf_op jit(solution)/shard_map/multiply/pallas_call | solution.py:193
  44.9 6.7 %collective-permute-start.2 = (f32[8,4,24,256]{3,2,1,0:T(8,128)S(1)}, f32[8,4,24,256]{3,2,1,0:T(8,128)S(1)}, u32[]{:S(2)}, u32[]{:S(2)}) collective-permute-start(f32[8,4,24,256]{3,2,1,0:T(8,128)S(1)} %get-tuple-element.12), channel_id=1, source_target_pairs={{0,1},{1,0},{2,3},{3,2},{4,5},{5,4},{6,7},{7,6},{8,9},{9,8},{10,11... | collective-permute-start | bytes 2359304 | tf_op jit(solution)/shard_map/ppermute | solution.py:237
  51.7 1.9 %collective-permute-done.2 = f32[8,4,24,256]{3,2,1,0:T(8,128)S(1)} collective-permute-done((f32[8,4,24,256]{3,2,1,0:T(8,128)S(1)}, f32[8,4,24,256]{3,2,1,0:T(8,128)S(1)}, u32[]{:S(2)}, u32[]{:S(2)}) %collective-permute-start.2) | collective-permute-done | bytes 786464 | tf_op jit(solution)/shard_map/ppermute | solution.py:237
  53.6 0.1 add.17
  53.7 25.4 %all_to_all.20 = f32[32,24,256]{2,1,0:T(8,128)S(1)} all-to-all(f32[32,24,256]{2,1,0:T(8,128)S(1)} %bitcast.23), channel_id=1, replica_groups=mesh['z'=12,'x'=4,'y'=8,'core'=2] {'y','x'}, dimensions={0} | all-to-all | bytes 1572864 | tf_op jit(solution)/shard_map/all_to_all | solution.py:216
  79.1 0.1 reduce_sum.9
  79.2 0.1 copy.10
  79.3 0.1 reshape.77
  79.3 24.8 %all_to_all.21 = f32[12,8,256]{2,1,0:T(8,128)S(1)} all-to-all(f32[12,8,256]{2,1,0:T(8,128)S(1)} %reshape.77), channel_id=1, replica_groups=mesh['z'=12,'x'=4,'y'=8,'core'=2] {'z'}, dimensions={0} | all-to-all | bytes 196608 | tf_op jit(solution)/shard_map/all_to_all | solution.py:216
  104.1 0.2 fusion
  104.4 14.4 %all_to_all.22 = f32[16,2,256]{2,1,0:T(2,128)S(1)} all-to-all(f32[16,2,256]{2,1,0:T(2,128)S(1)} %copy.12), channel_id=1, replica_groups=mesh['z'=12,'x'=4,'y'=8,'core'=2] {'core','y'}, dimensions={0} | all-to-all | bytes 65536 | tf_op jit(solution)/shard_map/all_to_all | solution.py:216
  118.8 0.6 copy.16
  (3 shorter events, 0.1 us)
Async XLA Ops:
  2.0 32.6 %all-to-all-start = ((f32[8,8,4096]{2,1,0:T(8,128)}), f32[8,8,4096]{2,1,0:T(8,128)S(1)}, u32[]{:S(2)}, u32[]{:S(2)}) async-start(f32[8,8,4096]{2,1,0:T(8,128)} %repeat.1), calls=%async_computation | async-start | bytes 2097152 | tf_op jit(solution)/shard_map/all_to_all | solution.py:216
  9.6 11.8 %collective-permute-start = (f32[64,4096]{1,0:T(8,128)}, f32[64,4096]{1,0:T(8,128)S(1)}, u32[]{:S(2)}, u32[]{:S(2)}) collective-permute-start(f32[64,4096]{1,0:T(8,128)} %bitcast.20), channel_id=1, source_target_pairs={{0,1},{1,0},{2,3},{3,2},{4,5},{5,4},{6,7},{7,6},{8,9},{9,8},{10,11... | collective-permute-start | bytes 3145736 | tf_op jit(solution)/shard_map/ppermute | solution.py:233
  18.7 9.9 %collective-permute-start.1 = (s32[2,1024]{1,0:T(2,128)S(1)}, s32[2,1024]{1,0:T(2,128)S(1)}, u32[]{:S(2)}, u32[]{:S(2)}) collective-permute-start(s32[2,1024]{1,0:T(2,128)S(1)} %pad_add_fusion.own_tasks_hbm), channel_id=1, source_target_pairs={{0,1},{1,0},{2,3},{3,2},{4,5},{5,4},{6,7},{7,6},{8,9},{9,8},{10,11... | collective-permute-start | bytes 24584 | tf_op jit(solution)/shard_map/ppermute | solution.py:230
  21.4 1.2 %copy-start.1 = (f32[1,1,64,4096]{3,2,1,0:T(8,128)S(1)}, f32[1,1,64,4096]{3,2,1,0:T(8,128)}, u32[]{:S(2)}) copy-start(f32[1,1,64,4096]{3,2,1,0:T(8,128)} %param.6) | copy-start | bytes 3145732
  26.6 1.9 %copy-start = (bf16[128,128,128]{2,1,0:T(8,128)(2,1)}, bf16[128,128,128]{2,1,0:T(8,128)(2,1)S(1)}, u32[]{:S(2)}) copy-start(bf16[128,128,128]{2,1,0:T(8,128)(2,1)S(1)} %split_rights.1.parts_hbm) | copy-start | bytes 12582916
  44.9 8.6 %collective-permute-start.2 = (f32[8,4,24,256]{3,2,1,0:T(8,128)S(1)}, f32[8,4,24,256]{3,2,1,0:T(8,128)S(1)}, u32[]{:S(2)}, u32[]{:S(2)}) collective-permute-start(f32[8,4,24,256]{3,2,1,0:T(8,128)S(1)} %get-tuple-element.12), channel_id=1, source_target_pairs={{0,1},{1,0},{2,3},{3,2},{4,5},{5,4},{6,7},{7,6},{8,9},{9,8},{10,11... | collective-permute-start | bytes 2359304 | tf_op jit(solution)/shard_map/ppermute | solution.py:237

commit v5 on v4

--- a/solution.py
+++ b/solution.py
@@ -121,11 +121,12 @@
         x = flat_ref[pl.ds(pl.multiple_of(k * FLAT, 8), ROWS), :]
         coarse = x.astype(jnp.bfloat16).astype(jnp.float32)
         fine = x - coarse
-        lhs_ref[k, :ROWS, :] = jnp.where(mask, coarse, pltpu.roll(fine, BS, 1)).astype(jnp.bfloat16)
-        lhs_ref[k, ROWS:, :] = jnp.where(mask, pltpu.roll(coarse, BS, 1), fine).astype(jnp.bfloat16)
-        return carry
-
-    lax.fori_loop(0, count, cut, 0, unroll=8)
+        turned = pltpu.roll(jnp.where(mask, fine, coarse), BS, 1)
+        lhs_ref[k, :ROWS, :] = jnp.where(mask, coarse, turned).astype(jnp.bfloat16)
+        lhs_ref[k, ROWS:, :] = jnp.where(mask, turned, fine).astype(jnp.bfloat16)
+        return carry
+
+    lax.fori_loop(0, count, cut, 0, unroll=16)
     for copy in copies:
         copy.wait()
 
@@ -151,7 +152,7 @@
                     acc1[tasks_ref[1, t + 1]] += part
         return carry
 
-    lax.fori_loop(0, count, one_block, 0, unroll=16)
+    lax.fori_loop(0, count, one_block, 0, unroll=32)
 
     _, columns, run = mine_ref.shape[:3]
     capacity = CAPACITY
@@ -160,12 +161,12 @@
         owner = s // capacity
         spot = (owner % columns) * run + (owner // columns) * capacity + s % capacity
         low, high = acc0[s], acc1[s]
-        even = low[:ROWS] + pltpu.roll(high[:ROWS], BS, 1)
-        odd = pltpu.roll(low[ROWS:], BS, 1) + high[ROWS:]
-        nat_ref[pl.ds(pl.multiple_of(spot * FLAT, 8), ROWS), :] = jnp.where(mask, even, odd)
-        return carry
-
-    lax.fori_loop(0, slot_count, fold, 0, unroll=16)
+        straight = jnp.where(mask, low[:ROWS], high[ROWS:])
+        turned = pltpu.roll(jnp.where(mask, low[ROWS:], high[:ROWS]), BS, 1)
+        nat_ref[pl.ds(pl.multiple_of(spot * FLAT, 8), ROWS), :] = straight + turned
+        return carry
+
+    lax.fori_loop(0, slot_count, fold, 0, unroll=32)
 
     tiles = ROWS // (2 * chips)
 

time: 120 us -> 120 us (level)
  no operation moved by 1% of the time
where the time goes in v5:
time: 120 us; the launch traced here: 119 us
  blocking collectives  64.6 us (54%)
  starting transfers between devices  24.7 us (21%)
  Pallas kernels  16 us (13%)
  waiting for transfers between devices  7.87 us (7%)
  local copies, waits for them, and re-layouts  4.04 us (3%)
  other arithmetic  1.61 us (1%)
    all_to_all x3, blocking collectives, exchange(): return lax.all_to_all(x, axis, split_axis=0, concat_axis=0, tiled=True)  64.6 us
    pallas_call x1, Pallas kernels, products(): pl.pallas_call(multiply, out_shape=(out, out), in_specs=[smem, anywhere,...  10.1 us
    ppermute x1, starting transfers between devices, local(): parts = prepare(rights, lax.ppermute(rights, 'core', SWAP))  8.34 us
    all_to_all x1, starting transfers between devices, exchange(): return lax.all_to_all(x, axis, split_axis=0, concat_axis=0, tiled=True)  7.66 us
    ppermute x1, starting transfers between devices, local(): mine = mine + lax.ppermute(other, 'core', SWAP)  6.74 us
    all_to_all x1, waiting for transfers between devices, exchange(): return lax.all_to_all(x, axis, split_axis=0, concat_axis=0, tiled=True)  5.98 us
    pallas_call x1, Pallas kernels, prepare(): pl.pallas_call(split_rights, out_shape=jax.ShapeDtypeStruct((2 * count, 2...  3.92 us
    unnamed x5, local copies, waits for them, and re-layouts  3.76 us
  transfers between devices with their start and end apart: 4, of which 2 were waited for; matrix products, arithmetic and copies ran while one was open for 1% of the time, Pallas kernels for 3%

profile of v5, /device:TPU:1, one launch (start us, length us, event | category | flops | bytes accessed | tf_op | source)
XLA Modules:
  0.0 119.1 jit_solution(3288719105815319757)
XLA Ops:
  0.0 2.0 %repeat.1 = f32[8,8,4096]{2,1,0:T(8,128)} custom-call(f32[8,4096]{1,0:T(8,128)} %bitcast.25), custom_call_target="tpu_custom_call" | custom-call | tf_op jit(solution)/shard_map/repeat/pallas_call | solution.py:75
  2.0 7.7 %all-to-all-start = ((f32[8,8,4096]{2,1,0:T(8,128)}), f32[8,8,4096]{2,1,0:T(8,128)S(1)}, u32[]{:S(2)}, u32[]{:S(2)}) async-start(f32[8,8,4096]{2,1,0:T(8,128)} %repeat.1), calls=%async_computation | async-start | bytes 2097152 | tf_op jit(solution)/shard_map/all_to_all | solution.py:217
  9.6 8.3 %collective-permute-start = (f32[64,4096]{1,0:T(8,128)}, f32[64,4096]{1,0:T(8,128)S(1)}, u32[]{:S(2)}, u32[]{:S(2)}) collective-permute-start(f32[64,4096]{1,0:T(8,128)} %bitcast.20), channel_id=1, source_target_pairs={{0,1},{1,0},{2,3},{3,2},{4,5},{5,4},{6,7},{7,6},{8,9},{9,8},{10,11... | collective-permute-start | bytes 3145736 | tf_op jit(solution)/shard_map/ppermute | solution.py:234
  18.0 0.7 pad_add_fusion.own_tasks_hbm
  18.7 1.9 %collective-permute-start.1 = (s32[2,1024]{1,0:T(2,128)S(1)}, s32[2,1024]{1,0:T(2,128)S(1)}, u32[]{:S(2)}, u32[]{:S(2)}) collective-permute-start(s32[2,1024]{1,0:T(2,128)S(1)} %pad_add_fusion.own_tasks_hbm), channel_id=1, source_target_pairs={{0,1},{1,0},{2,3},{3,2},{4,5},{5,4},{6,7},{7,6},{8,9},{9,8},{10,11... | collective-permute-start | bytes 24584 | tf_op jit(solution)/shard_map/ppermute | solution.py:231
  20.6 0.1 reshape.72
  20.7 0.7 compare_convert_fusion
  21.4 0.0 collective-permute-done.twin_ref
  21.4 0.0 copy-start.1
  21.5 1.2 %copy-done.1 = f32[1,1,64,4096]{3,2,1,0:T(8,128)S(1)} copy-done((f32[1,1,64,4096]{3,2,1,0:T(8,128)S(1)}, f32[1,1,64,4096]{3,2,1,0:T(8,128)}, u32[]{:S(2)}) %copy-start.1) | copy-done | bytes 1048600
  22.7 3.9 %split_rights.1.parts_hbm = bf16[128,128,128]{2,1,0:T(8,128)(2,1)S(1)} custom-call(f32[64,4096]{1,0:T(8,128)S(1)} %bitcast.21, f32[64,4096]{1,0:T(8,128)S(1)} %collective-permute-done.twin_ref), custom_call_target="tpu_custom_call" | custom-call | flops 4194304 | bytes 6291456 | tf_op jit(solution)/shard_map/split_rights/pallas_call | solution.py:54
  26.6 0.0 copy-start
  26.6 1.9 %copy-done = bf16[128,128,128]{2,1,0:T(8,128)(2,1)} copy-done((bf16[128,128,128]{2,1,0:T(8,128)(2,1)}, bf16[128,128,128]{2,1,0:T(8,128)(2,1)S(1)}, u32[]{:S(2)}) %copy-start) | copy-done | bytes 4194328
  28.5 0.0 collective-permute-done.1.twin_tasks_hbm
  28.5 6.0 %all-to-all-done.left_ref = f32[8,8,4096]{2,1,0:T(8,128)S(1)} async-done(((f32[8,8,4096]{2,1,0:T(8,128)}), f32[8,8,4096]{2,1,0:T(8,128)S(1)}, u32[]{:S(2)}, u32[]{:S(2)}) %all-to-all-start) | async-done | bytes 1048608 | tf_op jit(solution)/shard_map/all_to_all | solution.py:217
  34.5 10.1 %multiply.15 = (f32[8,4,24,256]{3,2,1,0:T(8,128)S(1)}, f32[8,4,24,256]{3,2,1,0:T(8,128)S(1)}) custom-call(s32[1]{0:T(128)} %bitcast.3.core_ref, s32[2,1024]{1,0:T(2,128)S(1)} %pad_add_fusion.own_tasks_hbm, s32[2,1024]{1,0:T(2,128)S(1)} %collective-permute-done.1.twin_tasks_hbm, f32[8,8,4096]{2,1,0:T(8,128)S(1)} %all-to-all-done.left_ref, ...), custom_call_target="tpu_custom_call" | custom-call | flops 2147483648 | bytes 8388608 | tf_op jit(solution)/shard_map/multiply/pallas_call | solution.py:194
  44.6 6.7 %collective-permute-start.2 = (f32[8,4,24,256]{3,2,1,0:T(8,128)S(1)}, f32[8,4,24,256]{3,2,1,0:T(8,128)S(1)}, u32[]{:S(2)}, u32[]{:S(2)}) collective-permute-start(f32[8,4,24,256]{3,2,1,0:T(8,128)S(1)} %get-tuple-element.12), channel_id=1, source_target_pairs={{0,1},{1,0},{2,3},{3,2},{4,5},{5,4},{6,7},{7,6},{8,9},{9,8},{10,11... | collective-permute-start | bytes 2359304 | tf_op jit(solution)/shard_map/ppermute | solution.py:238
  51.4 1.9 %collective-permute-done.2 = f32[8,4,24,256]{3,2,1,0:T(8,128)S(1)} collective-permute-done((f32[8,4,24,256]{3,2,1,0:T(8,128)S(1)}, f32[8,4,24,256]{3,2,1,0:T(8,128)S(1)}, u32[]{:S(2)}, u32[]{:S(2)}) %collective-permute-start.2) | collective-permute-done | bytes 786464 | tf_op jit(solution)/shard_map/ppermute | solution.py:238
  53.2 0.1 add.17
  53.4 25.4 %all_to_all.20 = f32[32,24,256]{2,1,0:T(8,128)S(1)} all-to-all(f32[32,24,256]{2,1,0:T(8,128)S(1)} %bitcast.23), channel_id=1, replica_groups=mesh['z'=12,'x'=4,'y'=8,'core'=2] {'y','x'}, dimensions={0} | all-to-all | bytes 1572864 | tf_op jit(solution)/shard_map/all_to_all | solution.py:217
  78.8 0.1 reduce_sum.9
  78.9 0.1 copy.10
  79.0 0.1 reshape.77
  79.0 24.8 %all_to_all.21 = f32[12,8,256]{2,1,0:T(8,128)S(1)} all-to-all(f32[12,8,256]{2,1,0:T(8,128)S(1)} %reshape.77), channel_id=1, replica_groups=mesh['z'=12,'x'=4,'y'=8,'core'=2] {'z'}, dimensions={0} | all-to-all | bytes 196608 | tf_op jit(solution)/shard_map/all_to_all | solution.py:217
  103.8 0.2 fusion
  104.0 14.4 %all_to_all.22 = f32[16,2,256]{2,1,0:T(2,128)S(1)} all-to-all(f32[16,2,256]{2,1,0:T(2,128)S(1)} %copy.12), channel_id=1, replica_groups=mesh['z'=12,'x'=4,'y'=8,'core'=2] {'core','y'}, dimensions={0} | all-to-all | bytes 65536 | tf_op jit(solution)/shard_map/all_to_all | solution.py:217
  118.5 0.6 copy.16
  (3 shorter events, 0.1 us)
Async XLA Ops:
  2.0 32.6 %all-to-all-start = ((f32[8,8,4096]{2,1,0:T(8,128)}), f32[8,8,4096]{2,1,0:T(8,128)S(1)}, u32[]{:S(2)}, u32[]{:S(2)}) async-start(f32[8,8,4096]{2,1,0:T(8,128)} %repeat.1), calls=%async_computation | async-start | bytes 2097152 | tf_op jit(solution)/shard_map/all_to_all | solution.py:217
  9.6 11.8 %collective-permute-start = (f32[64,4096]{1,0:T(8,128)}, f32[64,4096]{1,0:T(8,128)S(1)}, u32[]{:S(2)}, u32[]{:S(2)}) collective-permute-start(f32[64,4096]{1,0:T(8,128)} %bitcast.20), channel_id=1, source_target_pairs={{0,1},{1,0},{2,3},{3,2},{4,5},{5,4},{6,7},{7,6},{8,9},{9,8},{10,11... | collective-permute-start | bytes 3145736 | tf_op jit(solution)/shard_map/ppermute | solution.py:234
  18.7 9.9 %collective-permute-start.1 = (s32[2,1024]{1,0:T(2,128)S(1)}, s32[2,1024]{1,0:T(2,128)S(1)}, u32[]{:S(2)}, u32[]{:S(2)}) collective-permute-start(s32[2,1024]{1,0:T(2,128)S(1)} %pad_add_fusion.own_tasks_hbm), channel_id=1, source_target_pairs={{0,1},{1,0},{2,3},{3,2},{4,5},{5,4},{6,7},{7,6},{8,9},{9,8},{10,11... | collective-permute-start | bytes 24584 | tf_op jit(solution)/shard_map/ppermute | solution.py:231
  21.4 1.2 %copy-start.1 = (f32[1,1,64,4096]{3,2,1,0:T(8,128)S(1)}, f32[1,1,64,4096]{3,2,1,0:T(8,128)}, u32[]{:S(2)}) copy-start(f32[1,1,64,4096]{3,2,1,0:T(8,128)} %param.6) | copy-start | bytes 3145732
  26.6 1.9 %copy-start = (bf16[128,128,128]{2,1,0:T(8,128)(2,1)}, bf16[128,128,128]{2,1,0:T(8,128)(2,1)S(1)}, u32[]{:S(2)}) copy-start(bf16[128,128,128]{2,1,0:T(8,128)(2,1)S(1)} %split_rights.1.parts_hbm) | copy-start | bytes 12582916
  44.6 8.6 %collective-permute-start.2 = (f32[8,4,24,256]{3,2,1,0:T(8,128)S(1)}, f32[8,4,24,256]{3,2,1,0:T(8,128)S(1)}, u32[]{:S(2)}, u32[]{:S(2)}) collective-permute-start(f32[8,4,24,256]{3,2,1,0:T(8,128)S(1)} %get-tuple-element.12), channel_id=1, source_target_pairs={{0,1},{1,0},{2,3},{3,2},{4,5},{5,4},{6,7},{7,6},{8,9},{9,8},{10,11... | collective-permute-start | bytes 2359304 | tf_op jit(solution)/shard_map/ppermute | solution.py:238

commit v6 on v5

--- a/solution.py
+++ b/solution.py
@@ -56,7 +56,7 @@
         out_shape=jax.ShapeDtypeStruct((2 * count, 2 * BS, 128), jnp.bfloat16),
         in_specs=[pl.BlockSpec(memory_space=pltpu.VMEM)] * 2,
         out_specs=pl.BlockSpec(memory_space=pltpu.VMEM),
-        scratch_shapes=[pltpu.VMEM((2 * count * BS, 128), jnp.float32)],
+        scratch_shapes=[pltpu.VMEM(((2 * count + 8) * BS, 128), jnp.float32)],
         compiler_params=pltpu.CompilerParams(vmem_limit_bytes=VMEM_LIMIT),
         cost_estimate=pl.CostEstimate(flops=16 * count * BLK, bytes_accessed=24 * count * BLK, transcendentals=0),
         name="split_rights",
@@ -200,11 +200,11 @@
             pltpu.SMEM(own_tasks.shape, jnp.int32),
             pltpu.SMEM(twin_tasks.shape, jnp.int32),
             pltpu.VMEM(parts.shape, parts.dtype),
-            pltpu.VMEM((chips * share * FLAT, 128), jnp.float32),
+            pltpu.VMEM(((chips * share + 8) * FLAT, 128), jnp.float32),
             pltpu.VMEM((chips * share, BS, 128), jnp.bfloat16),
             acc,
             acc,
-            pltpu.VMEM((slot_count * FLAT, 128), jnp.float32),
+            pltpu.VMEM(((slot_count + 8) * FLAT, 128), jnp.float32),
             pltpu.SemaphoreType.DMA((3,)),
         ],
         compiler_params=pltpu.CompilerParams(vmem_limit_bytes=VMEM_LIMIT),

time: 120 us -> 120 us (level)
  no operation moved by 1% of the time
where the time goes in v6:
time: 120 us; the launch traced here: 119 us
  blocking collectives  64.6 us (54%)
  starting transfers between devices  24.7 us (21%)
  Pallas kernels  16 us (13%)
  waiting for transfers between devices  7.87 us (7%)
  local copies, waits for them, and re-layouts  4.04 us (3%)
  other arithmetic  1.61 us (1%)
    all_to_all x3, blocking collectives, exchange(): return lax.all_to_all(x, axis, split_axis=0, concat_axis=0, tiled=True)  64.6 us
    pallas_call x1, Pallas kernels, products(): pl.pallas_call(multiply, out_shape=(out, out), in_specs=[smem, anywhere,...  10.1 us
    ppermute x1, starting transfers between devices, local(): parts = prepare(rights, lax.ppermute(rights, 'core', SWAP))  8.34 us
    all_to_all x1, starting transfers between devices, exchange(): return lax.all_to_all(x, axis, split_axis=0, concat_axis=0, tiled=True)  7.66 us
    ppermute x1, starting transfers between devices, local(): mine = mine + lax.ppermute(other, 'core', SWAP)  6.74 us
    all_to_all x1, waiting for transfers between devices, exchange(): return lax.all_to_all(x, axis, split_axis=0, concat_axis=0, tiled=True)  5.98 us
    pallas_call x1, Pallas kernels, prepare(): pl.pallas_call(split_rights, out_shape=jax.ShapeDtypeStruct((2 * count, 2...  3.92 us
    unnamed x5, local copies, waits for them, and re-layouts  3.76 us
  transfers between devices with their start and end apart: 4, of which 2 were waited for; matrix products, arithmetic and copies ran while one was open for 1% of the time, Pallas kernels for 3%

profile of v6, /device:TPU:1, one launch (start us, length us, event | category | flops | bytes accessed | tf_op | source)
XLA Modules:
  0.0 119.1 jit_solution(13866646581847243839)
XLA Ops:
  0.0 2.0 %repeat.1 = f32[8,8,4096]{2,1,0:T(8,128)} custom-call(f32[8,4096]{1,0:T(8,128)} %bitcast.25), custom_call_target="tpu_custom_call" | custom-call | tf_op jit(solution)/shard_map/repeat/pallas_call | solution.py:75
  2.0 7.7 %all-to-all-start = ((f32[8,8,4096]{2,1,0:T(8,128)}), f32[8,8,4096]{2,1,0:T(8,128)S(1)}, u32[]{:S(2)}, u32[]{:S(2)}) async-start(f32[8,8,4096]{2,1,0:T(8,128)} %repeat.1), calls=%async_computation | async-start | bytes 2097152 | tf_op jit(solution)/shard_map/all_to_all | solution.py:217
  9.6 8.3 %collective-permute-start = (f32[64,4096]{1,0:T(8,128)}, f32[64,4096]{1,0:T(8,128)S(1)}, u32[]{:S(2)}, u32[]{:S(2)}) collective-permute-start(f32[64,4096]{1,0:T(8,128)} %bitcast.20), channel_id=1, source_target_pairs={{0,1},{1,0},{2,3},{3,2},{4,5},{5,4},{6,7},{7,6},{8,9},{9,8},{10,11... | collective-permute-start | bytes 3145736 | tf_op jit(solution)/shard_map/ppermute | solution.py:234
  18.0 0.7 pad_add_fusion.own_tasks_hbm
  18.7 1.9 %collective-permute-start.1 = (s32[2,1024]{1,0:T(2,128)S(1)}, s32[2,1024]{1,0:T(2,128)S(1)}, u32[]{:S(2)}, u32[]{:S(2)}) collective-permute-start(s32[2,1024]{1,0:T(2,128)S(1)} %pad_add_fusion.own_tasks_hbm), channel_id=1, source_target_pairs={{0,1},{1,0},{2,3},{3,2},{4,5},{5,4},{6,7},{7,6},{8,9},{9,8},{10,11... | collective-permute-start | bytes 24584 | tf_op jit(solution)/shard_map/ppermute | solution.py:231
  20.6 0.1 reshape.72
  20.7 0.7 compare_convert_fusion
  21.4 0.0 collective-permute-done.twin_ref
  21.4 0.0 copy-start.1
  21.5 1.2 %copy-done.1 = f32[1,1,64,4096]{3,2,1,0:T(8,128)S(1)} copy-done((f32[1,1,64,4096]{3,2,1,0:T(8,128)S(1)}, f32[1,1,64,4096]{3,2,1,0:T(8,128)}, u32[]{:S(2)}) %copy-start.1) | copy-done | bytes 1048600
  22.7 3.9 %split_rights.1.parts_hbm = bf16[128,128,128]{2,1,0:T(8,128)(2,1)S(1)} custom-call(f32[64,4096]{1,0:T(8,128)S(1)} %bitcast.21, f32[64,4096]{1,0:T(8,128)S(1)} %collective-permute-done.twin_ref), custom_call_target="tpu_custom_call" | custom-call | flops 4194304 | bytes 6291456 | tf_op jit(solution)/shard_map/split_rights/pallas_call | solution.py:54
  26.6 0.0 copy-start
  26.6 1.9 %copy-done = bf16[128,128,128]{2,1,0:T(8,128)(2,1)} copy-done((bf16[128,128,128]{2,1,0:T(8,128)(2,1)}, bf16[128,128,128]{2,1,0:T(8,128)(2,1)S(1)}, u32[]{:S(2)}) %copy-start) | copy-done | bytes 4194328
  28.5 0.0 collective-permute-done.1.twin_tasks_hbm
  28.5 6.0 %all-to-all-done.left_ref = f32[8,8,4096]{2,1,0:T(8,128)S(1)} async-done(((f32[8,8,4096]{2,1,0:T(8,128)}), f32[8,8,4096]{2,1,0:T(8,128)S(1)}, u32[]{:S(2)}, u32[]{:S(2)}) %all-to-all-start) | async-done | bytes 1048608 | tf_op jit(solution)/shard_map/all_to_all | solution.py:217
  34.5 10.1 %multiply.15 = (f32[8,4,24,256]{3,2,1,0:T(8,128)S(1)}, f32[8,4,24,256]{3,2,1,0:T(8,128)S(1)}) custom-call(s32[1]{0:T(128)} %bitcast.3.core_ref, s32[2,1024]{1,0:T(2,128)S(1)} %pad_add_fusion.own_tasks_hbm, s32[2,1024]{1,0:T(2,128)S(1)} %collective-permute-done.1.twin_tasks_hbm, f32[8,8,4096]{2,1,0:T(8,128)S(1)} %all-to-all-done.left_ref, ...), custom_call_target="tpu_custom_call" | custom-call | flops 2147483648 | bytes 8388608 | tf_op jit(solution)/shard_map/multiply/pallas_call | solution.py:194
  44.6 6.7 %collective-permute-start.2 = (f32[8,4,24,256]{3,2,1,0:T(8,128)S(1)}, f32[8,4,24,256]{3,2,1,0:T(8,128)S(1)}, u32[]{:S(2)}, u32[]{:S(2)}) collective-permute-start(f32[8,4,24,256]{3,2,1,0:T(8,128)S(1)} %get-tuple-element.12), channel_id=1, source_target_pairs={{0,1},{1,0},{2,3},{3,2},{4,5},{5,4},{6,7},{7,6},{8,9},{9,8},{10,11... | collective-permute-start | bytes 2359304 | tf_op jit(solution)/shard_map/ppermute | solution.py:238
  51.4 1.9 %collective-permute-done.2 = f32[8,4,24,256]{3,2,1,0:T(8,128)S(1)} collective-permute-done((f32[8,4,24,256]{3,2,1,0:T(8,128)S(1)}, f32[8,4,24,256]{3,2,1,0:T(8,128)S(1)}, u32[]{:S(2)}, u32[]{:S(2)}) %collective-permute-start.2) | collective-permute-done | bytes 786464 | tf_op jit(solution)/shard_map/ppermute | solution.py:238
  53.2 0.1 add.17
  53.4 25.4 %all_to_all.20 = f32[32,24,256]{2,1,0:T(8,128)S(1)} all-to-all(f32[32,24,256]{2,1,0:T(8,128)S(1)} %bitcast.23), channel_id=1, replica_groups=mesh['z'=12,'x'=4,'y'=8,'core'=2] {'y','x'}, dimensions={0} | all-to-all | bytes 1572864 | tf_op jit(solution)/shard_map/all_to_all | solution.py:217
  78.8 0.1 reduce_sum.9
  78.9 0.1 copy.10
  79.0 0.1 reshape.77
  79.0 24.8 %all_to_all.21 = f32[12,8,256]{2,1,0:T(8,128)S(1)} all-to-all(f32[12,8,256]{2,1,0:T(8,128)S(1)} %reshape.77), channel_id=1, replica_groups=mesh['z'=12,'x'=4,'y'=8,'core'=2] {'z'}, dimensions={0} | all-to-all | bytes 196608 | tf_op jit(solution)/shard_map/all_to_all | solution.py:217
  103.8 0.2 fusion
  104.0 14.4 %all_to_all.22 = f32[16,2,256]{2,1,0:T(2,128)S(1)} all-to-all(f32[16,2,256]{2,1,0:T(2,128)S(1)} %copy.12), channel_id=1, replica_groups=mesh['z'=12,'x'=4,'y'=8,'core'=2] {'core','y'}, dimensions={0} | all-to-all | bytes 65536 | tf_op jit(solution)/shard_map/all_to_all | solution.py:217
  118.5 0.6 copy.16
  (3 shorter events, 0.1 us)
Async XLA Ops:
  2.0 32.6 %all-to-all-start = ((f32[8,8,4096]{2,1,0:T(8,128)}), f32[8,8,4096]{2,1,0:T(8,128)S(1)}, u32[]{:S(2)}, u32[]{:S(2)}) async-start(f32[8,8,4096]{2,1,0:T(8,128)} %repeat.1), calls=%async_computation | async-start | bytes 2097152 | tf_op jit(solution)/shard_map/all_to_all | solution.py:217
  9.6 11.8 %collective-permute-start = (f32[64,4096]{1,0:T(8,128)}, f32[64,4096]{1,0:T(8,128)S(1)}, u32[]{:S(2)}, u32[]{:S(2)}) collective-permute-start(f32[64,4096]{1,0:T(8,128)} %bitcast.20), channel_id=1, source_target_pairs={{0,1},{1,0},{2,3},{3,2},{4,5},{5,4},{6,7},{7,6},{8,9},{9,8},{10,11... | collective-permute-start | bytes 3145736 | tf_op jit(solution)/shard_map/ppermute | solution.py:234
  18.7 9.9 %collective-permute-start.1 = (s32[2,1024]{1,0:T(2,128)S(1)}, s32[2,1024]{1,0:T(2,128)S(1)}, u32[]{:S(2)}, u32[]{:S(2)}) collective-permute-start(s32[2,1024]{1,0:T(2,128)S(1)} %pad_add_fusion.own_tasks_hbm), channel_id=1, source_target_pairs={{0,1},{1,0},{2,3},{3,2},{4,5},{5,4},{6,7},{7,6},{8,9},{9,8},{10,11... | collective-permute-start | bytes 24584 | tf_op jit(solution)/shard_map/ppermute | solution.py:231
  21.4 1.2 %copy-start.1 = (f32[1,1,64,4096]{3,2,1,0:T(8,128)S(1)}, f32[1,1,64,4096]{3,2,1,0:T(8,128)}, u32[]{:S(2)}) copy-start(f32[1,1,64,4096]{3,2,1,0:T(8,128)} %param.6) | copy-start | bytes 3145732
  26.6 1.9 %copy-start = (bf16[128,128,128]{2,1,0:T(8,128)(2,1)}, bf16[128,128,128]{2,1,0:T(8,128)(2,1)S(1)}, u32[]{:S(2)}) copy-start(bf16[128,128,128]{2,1,0:T(8,128)(2,1)S(1)} %split_rights.1.parts_hbm) | copy-start | bytes 12582916
  44.6 8.6 %collective-permute-start.2 = (f32[8,4,24,256]{3,2,1,0:T(8,128)S(1)}, f32[8,4,24,256]{3,2,1,0:T(8,128)S(1)}, u32[]{:S(2)}, u32[]{:S(2)}) collective-permute-start(f32[8,4,24,256]{3,2,1,0:T(8,128)S(1)} %get-tuple-element.12), channel_id=1, source_target_pairs={{0,1},{1,0},{2,3},{3,2},{4,5},{5,4},{6,7},{7,6},{8,9},{9,8},{10,11... | collective-permute-start | bytes 2359304 | tf_op jit(solution)/shard_map/ppermute | solution.py:238

commit v7 on v6

--- a/solution.py
+++ b/solution.py
@@ -166,7 +166,7 @@
         nat_ref[pl.ds(pl.multiple_of(spot * FLAT, 8), ROWS), :] = straight + turned
         return carry
 
-    lax.fori_loop(0, slot_count, fold, 0, unroll=32)
+    lax.fori_loop(0, slot_count, fold, 0, unroll=16)
 
     tiles = ROWS // (2 * chips)
 

time: 120 us -> 120 us (level)
  no operation moved by 1% of the time
where the time goes in v7:
time: 120 us; the launch traced here: 119 us
  blocking collectives  64.6 us (54%)
  starting transfers between devices  24.7 us (21%)
  Pallas kernels  15.9 us (13%)
  waiting for transfers between devices  7.87 us (7%)
  local copies, waits for them, and re-layouts  4.04 us (3%)
  other arithmetic  1.61 us (1%)
    all_to_all x3, blocking collectives, exchange(): return lax.all_to_all(x, axis, split_axis=0, concat_axis=0, tiled=True)  64.6 us
    pallas_call x1, Pallas kernels, products(): pl.pallas_call(multiply, out_shape=(out, out), in_specs=[smem, anywhere,...  10.1 us
    ppermute x1, starting transfers between devices, local(): parts = prepare(rights, lax.ppermute(rights, 'core', SWAP))  8.34 us
    all_to_all x1, starting transfers between devices, exchange(): return lax.all_to_all(x, axis, split_axis=0, concat_axis=0, tiled=True)  7.66 us
    ppermute x1, starting transfers between devices, local(): mine = mine + lax.ppermute(other, 'core', SWAP)  6.74 us
    all_to_all x1, waiting for transfers between devices, exchange(): return lax.all_to_all(x, axis, split_axis=0, concat_axis=0, tiled=True)  5.98 us
    pallas_call x1, Pallas kernels, prepare(): pl.pallas_call(split_rights, out_shape=jax.ShapeDtypeStruct((2 * count, 2...  3.92 us
    unnamed x5, local copies, waits for them, and re-layouts  3.76 us
  transfers between devices with their start and end apart: 4, of which 2 were waited for; matrix products, arithmetic and copies ran while one was open for 1% of the time, Pallas kernels for 3%

profile of v7, /device:TPU:1, one launch (start us, length us, event | category | flops | bytes accessed | tf_op | source)
XLA Modules:
  0.0 119.0 jit_solution(5993498363664648616)
XLA Ops:
  0.0 2.0 %repeat.1 = f32[8,8,4096]{2,1,0:T(8,128)} custom-call(f32[8,4096]{1,0:T(8,128)} %bitcast.25), custom_call_target="tpu_custom_call" | custom-call | tf_op jit(solution)/shard_map/repeat/pallas_call | solution.py:75
  2.0 7.7 %all-to-all-start = ((f32[8,8,4096]{2,1,0:T(8,128)}), f32[8,8,4096]{2,1,0:T(8,128)S(1)}, u32[]{:S(2)}, u32[]{:S(2)}) async-start(f32[8,8,4096]{2,1,0:T(8,128)} %repeat.1), calls=%async_computation | async-start | bytes 2097152 | tf_op jit(solution)/shard_map/all_to_all | solution.py:217
  9.6 8.3 %collective-permute-start = (f32[64,4096]{1,0:T(8,128)}, f32[64,4096]{1,0:T(8,128)S(1)}, u32[]{:S(2)}, u32[]{:S(2)}) collective-permute-start(f32[64,4096]{1,0:T(8,128)} %bitcast.20), channel_id=1, source_target_pairs={{0,1},{1,0},{2,3},{3,2},{4,5},{5,4},{6,7},{7,6},{8,9},{9,8},{10,11... | collective-permute-start | bytes 3145736 | tf_op jit(solution)/shard_map/ppermute | solution.py:234
  18.0 0.7 pad_add_fusion.own_tasks_hbm
  18.7 1.9 %collective-permute-start.1 = (s32[2,1024]{1,0:T(2,128)S(1)}, s32[2,1024]{1,0:T(2,128)S(1)}, u32[]{:S(2)}, u32[]{:S(2)}) collective-permute-start(s32[2,1024]{1,0:T(2,128)S(1)} %pad_add_fusion.own_tasks_hbm), channel_id=1, source_target_pairs={{0,1},{1,0},{2,3},{3,2},{4,5},{5,4},{6,7},{7,6},{8,9},{9,8},{10,11... | collective-permute-start | bytes 24584 | tf_op jit(solution)/shard_map/ppermute | solution.py:231
  20.6 0.1 reshape.72
  20.7 0.7 compare_convert_fusion
  21.4 0.0 collective-permute-done.twin_ref
  21.4 0.0 copy-start.1
  21.5 1.2 %copy-done.1 = f32[1,1,64,4096]{3,2,1,0:T(8,128)S(1)} copy-done((f32[1,1,64,4096]{3,2,1,0:T(8,128)S(1)}, f32[1,1,64,4096]{3,2,1,0:T(8,128)}, u32[]{:S(2)}) %copy-start.1) | copy-done | bytes 1048600
  22.7 3.9 %split_rights.1.parts_hbm = bf16[128,128,128]{2,1,0:T(8,128)(2,1)S(1)} custom-call(f32[64,4096]{1,0:T(8,128)S(1)} %bitcast.21, f32[64,4096]{1,0:T(8,128)S(1)} %collective-permute-done.twin_ref), custom_call_target="tpu_custom_call" | custom-call | flops 4194304 | bytes 6291456 | tf_op jit(solution)/shard_map/split_rights/pallas_call | solution.py:54
  26.6 0.0 copy-start
  26.6 1.9 %copy-done = bf16[128,128,128]{2,1,0:T(8,128)(2,1)} copy-done((bf16[128,128,128]{2,1,0:T(8,128)(2,1)}, bf16[128,128,128]{2,1,0:T(8,128)(2,1)S(1)}, u32[]{:S(2)}) %copy-start) | copy-done | bytes 4194328
  28.5 0.0 collective-permute-done.1.twin_tasks_hbm
  28.5 6.0 %all-to-all-done.left_ref = f32[8,8,4096]{2,1,0:T(8,128)S(1)} async-done(((f32[8,8,4096]{2,1,0:T(8,128)}), f32[8,8,4096]{2,1,0:T(8,128)S(1)}, u32[]{:S(2)}, u32[]{:S(2)}) %all-to-all-start) | async-done | bytes 1048608 | tf_op jit(solution)/shard_map/all_to_all | solution.py:217
  34.5 10.1 %multiply.15 = (f32[8,4,24,256]{3,2,1,0:T(8,128)S(1)}, f32[8,4,24,256]{3,2,1,0:T(8,128)S(1)}) custom-call(s32[1]{0:T(128)} %bitcast.3.core_ref, s32[2,1024]{1,0:T(2,128)S(1)} %pad_add_fusion.own_tasks_hbm, s32[2,1024]{1,0:T(2,128)S(1)} %collective-permute-done.1.twin_tasks_hbm, f32[8,8,4096]{2,1,0:T(8,128)S(1)} %all-to-all-done.left_ref, ...), custom_call_target="tpu_custom_call" | custom-call | flops 2147483648 | bytes 8388608 | tf_op jit(solution)/shard_map/multiply/pallas_call | solution.py:194
  44.6 6.7 %collective-permute-start.2 = (f32[8,4,24,256]{3,2,1,0:T(8,128)S(1)}, f32[8,4,24,256]{3,2,1,0:T(8,128)S(1)}, u32[]{:S(2)}, u32[]{:S(2)}) collective-permute-start(f32[8,4,24,256]{3,2,1,0:T(8,128)S(1)} %get-tuple-element.12), channel_id=1, source_target_pairs={{0,1},{1,0},{2,3},{3,2},{4,5},{5,4},{6,7},{7,6},{8,9},{9,8},{10,11... | collective-permute-start | bytes 2359304 | tf_op jit(solution)/shard_map/ppermute | solution.py:238
  51.3 1.9 %collective-permute-done.2 = f32[8,4,24,256]{3,2,1,0:T(8,128)S(1)} collective-permute-done((f32[8,4,24,256]{3,2,1,0:T(8,128)S(1)}, f32[8,4,24,256]{3,2,1,0:T(8,128)S(1)}, u32[]{:S(2)}, u32[]{:S(2)}) %collective-permute-start.2) | collective-permute-done | bytes 786464 | tf_op jit(solution)/shard_map/ppermute | solution.py:238
  53.2 0.1 add.17
  53.3 25.4 %all_to_all.20 = f32[32,24,256]{2,1,0:T(8,128)S(1)} all-to-all(f32[32,24,256]{2,1,0:T(8,128)S(1)} %bitcast.23), channel_id=1, replica_groups=mesh['z'=12,'x'=4,'y'=8,'core'=2] {'y','x'}, dimensions={0} | all-to-all | bytes 1572864 | tf_op jit(solution)/shard_map/all_to_all | solution.py:217
  78.8 0.1 reduce_sum.9
  78.9 0.1 copy.10
  78.9 0.1 reshape.77
  79.0 24.8 %all_to_all.21 = f32[12,8,256]{2,1,0:T(8,128)S(1)} all-to-all(f32[12,8,256]{2,1,0:T(8,128)S(1)} %reshape.77), channel_id=1, replica_groups=mesh['z'=12,'x'=4,'y'=8,'core'=2] {'z'}, dimensions={0} | all-to-all | bytes 196608 | tf_op jit(solution)/shard_map/all_to_all | solution.py:217
  103.8 0.2 fusion
  104.0 14.4 %all_to_all.22 = f32[16,2,256]{2,1,0:T(2,128)S(1)} all-to-all(f32[16,2,256]{2,1,0:T(2,128)S(1)} %copy.12), channel_id=1, replica_groups=mesh['z'=12,'x'=4,'y'=8,'core'=2] {'core','y'}, dimensions={0} | all-to-all | bytes 65536 | tf_op jit(solution)/shard_map/all_to_all | solution.py:217
  118.4 0.6 copy.16
  (3 shorter events, 0.1 us)
Async XLA Ops:
  2.0 32.6 %all-to-all-start = ((f32[8,8,4096]{2,1,0:T(8,128)}), f32[8,8,4096]{2,1,0:T(8,128)S(1)}, u32[]{:S(2)}, u32[]{:S(2)}) async-start(f32[8,8,4096]{2,1,0:T(8,128)} %repeat.1), calls=%async_computation | async-start | bytes 2097152 | tf_op jit(solution)/shard_map/all_to_all | solution.py:217
  9.6 11.8 %collective-permute-start = (f32[64,4096]{1,0:T(8,128)}, f32[64,4096]{1,0:T(8,128)S(1)}, u32[]{:S(2)}, u32[]{:S(2)}) collective-permute-start(f32[64,4096]{1,0:T(8,128)} %bitcast.20), channel_id=1, source_target_pairs={{0,1},{1,0},{2,3},{3,2},{4,5},{5,4},{6,7},{7,6},{8,9},{9,8},{10,11... | collective-permute-start | bytes 3145736 | tf_op jit(solution)/shard_map/ppermute | solution.py:234
  18.7 9.9 %collective-permute-start.1 = (s32[2,1024]{1,0:T(2,128)S(1)}, s32[2,1024]{1,0:T(2,128)S(1)}, u32[]{:S(2)}, u32[]{:S(2)}) collective-permute-start(s32[2,1024]{1,0:T(2,128)S(1)} %pad_add_fusion.own_tasks_hbm), channel_id=1, source_target_pairs={{0,1},{1,0},{2,3},{3,2},{4,5},{5,4},{6,7},{7,6},{8,9},{9,8},{10,11... | collective-permute-start | bytes 24584 | tf_op jit(solution)/shard_map/ppermute | solution.py:231
  21.4 1.2 %copy-start.1 = (f32[1,1,64,4096]{3,2,1,0:T(8,128)S(1)}, f32[1,1,64,4096]{3,2,1,0:T(8,128)}, u32[]{:S(2)}) copy-start(f32[1,1,64,4096]{3,2,1,0:T(8,128)} %param.6) | copy-start | bytes 3145732
  26.6 1.9 %copy-start = (bf16[128,128,128]{2,1,0:T(8,128)(2,1)}, bf16[128,128,128]{2,1,0:T(8,128)(2,1)S(1)}, u32[]{:S(2)}) copy-start(bf16[128,128,128]{2,1,0:T(8,128)(2,1)S(1)} %split_rights.1.parts_hbm) | copy-start | bytes 12582916
  44.6 8.6 %collective-permute-start.2 = (f32[8,4,24,256]{3,2,1,0:T(8,128)S(1)}, f32[8,4,24,256]{3,2,1,0:T(8,128)S(1)}, u32[]{:S(2)}, u32[]{:S(2)}) collective-permute-start(f32[8,4,24,256]{3,2,1,0:T(8,128)S(1)} %get-tuple-element.12), channel_id=1, source_target_pairs={{0,1},{1,0},{2,3},{3,2},{4,5},{5,4},{6,7},{7,6},{8,9},{9,8},{10,11... | collective-permute-start | bytes 2359304 | tf_op jit(solution)/shard_map/ppermute | solution.py:238
